TPU v7x, 32 devices: a whole 2x2x4 slice. The times are simulated.
32 devices in a mesh: gx: 4 (over z), gy: 8 (over y, x, core).
Axes of the slice: x: 2, y: 2, z: 4, core: 2. Of those that a mesh axis runs over, the one named last changes fastest.
Arguments:
- flow_state: float32 [4, 32, 64, 128], P(None, 'gx', 'gy'), may hold values from -4.5 to 4.5, as said below
- building_height: int32 [4, 8], P('gx', 'gy'), may hold values from 0 to 8
- pressure_old: float32 [32, 64, 128], P('gx', 'gy'), may hold values from -0.3 to 0.3
Outputs:
- new_state: float32 [4, 32, 64, 128], P(None, 'gx', 'gy')
- pressure: float32 [32, 64, 128], P('gx', 'gy')
Inputs may be any that keep to these rules, and one draw needn't show every extreme that they name: `flow_state`: velocity and temperature fluctuations whose size varies across the district.
All inputs are finite; a program needn't handle non-finite values.
Results may differ from a plain program's by a relative error of at most 0.0003.
Values sent between devices are 32-bit elements; how exact they have to be, the bound alone decides.
A program may use at most 64 MiB of HBM per device.

v0:
```python
import math

import jax
import jax.numpy as jnp
import numpy as np
from jax import lax
from jax.sharding import PartitionSpec as P

ITERS = 2


HIGHEST = lax.Precision.HIGHEST
viscosity = 0.05
time_step = 0.01
drag_strength = 20.0
heating = 40.0
buoyancy = 10.0
helmholtz_shift = 0.001
local_shift = 0.5
coarse_shift = 0.02
gll_points = (
    -1.0,
    -0.8717401485096066,
    -0.5917001814331423,
    -0.2092992179024789,
    0.2092992179024789,
    0.5917001814331423,
    0.8717401485096066,
    1.0,
)


def padded_2(cells, sides, width):
    for axis, dim in sides:
        count = lax.axis_size(axis)
        head = lax.slice_in_dim(cells, 0, width, axis=dim)
        tail = lax.slice_in_dim(cells, cells.shape[dim] - width, cells.shape[dim], axis=dim)
        cells = jnp.concatenate(
            [
                lax.ppermute(tail, axis, [(i, (i + 1) % count) for i in range(count)]),
                cells,
                lax.ppermute(head, axis, [((i + 1) % count, i) for i in range(count)]),
            ],
            axis=dim,
        )
    return cells


def legendre_seven(points):
    squared = points * points
    return points * (((429.0 * squared - 693.0) * squared + 315.0) * squared - 35.0) / 16.0


def jacobi_eigen(matrix):
    current = np.array(matrix)
    basis = np.eye(8)
    for rounds in range(12):
        for first in range(7):
            for second in range(first + 1, 8):
                rotation_angle = 0.5 * math.atan2(
                    2.0 * float(current[first, second]),
                    float(current[second, second] - current[first, first]),
                )
                cosine = math.cos(rotation_angle)
                sine = math.sin(rotation_angle)
                rotation = np.eye(8)
                rotation[first, first] = cosine
                rotation[second, second] = cosine
                rotation[first, second] = sine
                rotation[second, first] = -sine
                current = rotation.T @ current @ rotation
                basis = basis @ rotation
    return (np.sum(current * np.eye(8), axis=0), basis)


def gll_tables():
    gll_nodes = np.array(gll_points)
    values = legendre_seven(gll_nodes)
    weights = 2.0 / (56.0 * values * values)
    differ = gll_nodes[:, None] - gll_nodes[None, :] + np.eye(8)
    derivative = values[:, None] / values[None, :] / differ * (1.0 - np.eye(8))
    derivative = (
        derivative + np.eye(8) * np.array([-14.0, 0.0, 0.0, 0.0, 0.0, 0.0, 0.0, 14.0])[None, :]
    )
    stiffness = derivative.T @ (weights[:, None] * derivative)
    scaled = stiffness / np.sqrt(np.outer(weights, weights))
    scaled = 0.5 * (scaled + scaled.T)
    eigen_values, eigen_vectors = jacobi_eigen(scaled)
    eigen_basis = eigen_vectors / np.sqrt(weights)[:, None]
    return (gll_nodes, weights, derivative, eigen_basis, np.maximum(eigen_values, 0.0))


def tables():
    return tuple((jnp.asarray(table, dtype=jnp.float32) for table in gll_tables()))


def along_x(field, matrix):
    first, second, third, fourth = field.shape
    blocks = field.reshape(first, second // 8, 8, third, fourth)
    return jnp.einsum("ij,cejyz->ceiyz", matrix, blocks, precision=HIGHEST).reshape(field.shape)


def along_y(field, matrix):
    first, second, third, fourth = field.shape
    blocks = field.reshape(first, second, third // 8, 8, fourth)
    return jnp.einsum("ij,cxejz->cxeiz", matrix, blocks, precision=HIGHEST).reshape(field.shape)


def along_z(field, matrix):
    first, second, third, fourth = field.shape
    banded = jnp.kron(jnp.eye(fourth // 8, dtype=jnp.float32), matrix)
    rows = field.reshape(first * second * third, fourth)
    return jnp.dot(rows, banded.T, precision=HIGHEST).reshape(field.shape)


def weight_grid(weights, width, depth, height):
    return (
        jnp.tile(weights, width // 8)[:, None, None]
        * jnp.tile(weights, depth // 8)[None, :, None]
        * jnp.tile(weights, height // 8)[None, None, :]
    )


def face_counts(count):
    index = jnp.arange(count, dtype=jnp.int32) % 8
    return jnp.where((index == 0) | (index == 7), 2.0, 1.0).astype(jnp.float32)


def multiplicity(width, depth, height):
    vertical_index = jnp.arange(height, dtype=jnp.int32)
    ends = (vertical_index == 0) | (vertical_index == height - 1)
    vertical = jnp.where(ends, 1.0, face_counts(height))
    return (
        face_counts(width)[:, None, None]
        * face_counts(depth)[None, :, None]
        * vertical[None, None, :]
    )


def canopy_mask(building_height, height):
    column = jnp.repeat(jnp.repeat(building_height, 8, axis=0), 8, axis=1)
    layer = jnp.arange(height, dtype=jnp.int32) // 8
    return (layer[None, None, :] < column[:, :, None]).astype(jnp.float32)


def stiffness_action(field, mass, derivative):
    term = along_x(mass * along_x(field, derivative), derivative.T)
    term = term + along_y(mass * along_y(field, derivative), derivative.T)
    return term + along_z(mass * along_z(field, derivative), derivative.T)


def pair_z(field):
    first, second, third, fourth = field.shape
    index = jnp.arange(fourth, dtype=jnp.int32)
    source_index = index[:, None]
    target_index = index[None, :]
    upper = (source_index % 8 == 7) & (target_index == source_index + 1)
    lower = (source_index % 8 == 0) & (target_index == source_index - 1) & (source_index > 0)
    joining = ((source_index == target_index) | upper | lower).astype(jnp.float32)
    rows = field.reshape(first * second * third, fourth)
    return jnp.dot(rows, joining, precision=HIGHEST).reshape(field.shape)


def pair_x_padded(padded):
    first, second, third, fourth = padded.shape
    inner = padded[:, 1:-1].reshape(first, (second - 2) // 8, 8, third, fourth)
    lasts = jnp.concatenate([padded[:, :1], inner[:, :, 7]], axis=1)
    starts = jnp.concatenate([inner[:, :, 0], padded[:, -1:]], axis=1)
    sums = lasts + starts
    joined = jnp.concatenate([sums[:, :-1, None], inner[:, :, 1:7], sums[:, 1:, None]], axis=2)
    return joined.reshape(first, second - 2, third, fourth)


def pair_y_padded(padded):
    first, second, third, fourth = padded.shape
    inner = padded[:, :, 1:-1].reshape(first, second, (third - 2) // 8, 8, fourth)
    lasts = jnp.concatenate([padded[:, :, :1], inner[:, :, :, 7]], axis=2)
    starts = jnp.concatenate([inner[:, :, :, 0], padded[:, :, -1:]], axis=2)
    sums = lasts + starts
    joined = jnp.concatenate(
        [sums[:, :, :-1, None], inner[:, :, :, 1:7], sums[:, :, 1:, None]], axis=3
    )
    return joined.reshape(first, second, third - 2, fourth)


def assemble(field):
    padded = padded_2(field, (("gx", 1), ("gy", 2)), 1)
    return pair_z(pair_y_padded(pair_x_padded(padded)))


def local_solve(field, eigen_basis, eigen_values):
    first, width, depth, height = field.shape
    spectrum = (
        jnp.tile(eigen_values, width // 8)[:, None, None]
        + jnp.tile(eigen_values, depth // 8)[None, :, None]
        + jnp.tile(eigen_values, height // 8)[None, None, :]
    )
    inverse = eigen_basis.T
    modal = along_z(along_y(along_x(field, inverse), inverse), inverse)
    modal = modal / (spectrum + local_shift)
    return along_z(along_y(along_x(modal, eigen_basis), eigen_basis), eigen_basis)


def interpolation(width, gll_nodes):
    count = width // 8
    columns = count + 1
    position = jnp.tile(gll_nodes, count)
    element = jnp.arange(width, dtype=jnp.int32) // 8
    following = element + 1
    target = jnp.arange(columns, dtype=jnp.int32)[None, :]
    left = jnp.where(target == element[:, None], (1.0 - position)[:, None] / 2.0, 0.0)
    right = jnp.where(target == following[:, None], (1.0 + position)[:, None] / 2.0, 0.0)
    return left + right


def restrict(field, across, along, vertical):
    reduced = jnp.einsum("xa,xyz->ayz", across, field, precision=HIGHEST)
    reduced = jnp.einsum("yb,ayz->abz", along, reduced, precision=HIGHEST)
    return jnp.einsum("zc,abz->abc", vertical, reduced, precision=HIGHEST)


def prolong(coarse, across, along, vertical):
    fine = jnp.einsum("zc,abc->abz", vertical, coarse, precision=HIGHEST)
    fine = jnp.einsum("yb,abz->ayz", along, fine, precision=HIGHEST)
    return jnp.einsum("xa,ayz->xyz", across, fine, precision=HIGHEST)


def spectral_tables(count):
    index = jnp.arange(count, dtype=jnp.int32)
    angle = 2.0 * np.pi / count * (index[:, None] * index[None, :] % count).astype(jnp.float32)
    hartley = (jnp.cos(angle) + jnp.sin(angle)) / np.sqrt(count)
    eigen = 2.0 - 2.0 * jnp.cos(2.0 * np.pi / count * index.astype(jnp.float32))
    return (hartley.astype(jnp.float32), eigen.astype(jnp.float32))


def cosine_tables(count):
    index = jnp.arange(count, dtype=jnp.int32).astype(jnp.float32)
    angle = np.pi / count * (index[:, None] + 0.5) * index[None, :]
    norms = jnp.where(index == 0, np.sqrt(1.0 / count), np.sqrt(2.0 / count))
    basis = jnp.cos(angle) * norms[None, :]
    eigen = 2.0 - 2.0 * jnp.cos(np.pi / count * index)
    return (basis.astype(jnp.float32), eigen.astype(jnp.float32))


def coarse_solve_levels(grid):
    levels, first, second = grid.shape
    hartley_x, eigen_x = spectral_tables(first)
    hartley_y, eigen_y = spectral_tables(second)
    cosine_z, eigen_z = cosine_tables(levels)
    modes = jnp.einsum("ai,kij->kaj", hartley_x, grid, precision=HIGHEST)
    modes = jnp.einsum("bj,kaj->kab", hartley_y, modes, precision=HIGHEST)
    modes = jnp.einsum("kc,kab->cab", cosine_z, modes, precision=HIGHEST)
    modes = modes / (
        2.0 * (eigen_z[:, None, None] + eigen_x[None, :, None] + eigen_y[None, None, :])
        + coarse_shift
    )
    values = jnp.einsum("kc,cab->kab", cosine_z, modes, precision=HIGHEST)
    values = jnp.einsum("bj,kab->kaj", hartley_y, values, precision=HIGHEST)
    return jnp.einsum("ai,kaj->kij", hartley_x, values, precision=HIGHEST)


def coarse_whole(piece):
    rows, columns, levels = piece.shape
    gathered = lax.all_gather(
        piece.reshape(1, rows * columns * levels), ("gx", "gy"), axis=0, tiled=True
    )
    parts_x = lax.axis_size("gx")
    parts_y = lax.axis_size("gy")
    grid = gathered.reshape(parts_x, parts_y, rows, columns, levels).transpose(4, 2, 3, 0, 1)
    inner_x = rows - 1
    inner_y = columns - 1
    core = grid[:, :inner_x, :inner_y]
    core = core.at[:, 0].add(jnp.roll(grid[:, inner_x, :inner_y], 1, axis=2))
    core = core.at[:, :, 0].add(jnp.roll(grid[:, :inner_x, inner_y], 1, axis=3))
    core = core.at[:, 0, 0].add(jnp.roll(grid[:, inner_x, inner_y], (1, 1), axis=(1, 2)))
    whole = core.transpose(0, 3, 1, 4, 2).reshape(levels, parts_x * inner_x, parts_y * inner_y)
    solution = coarse_solve_levels(whole)
    extended = jnp.concatenate([solution, solution[:, :inner_x]], axis=1)
    extended = jnp.concatenate([extended, extended[:, :, :inner_y]], axis=2)
    start_x = lax.axis_index("gx") * inner_x
    start_y = lax.axis_index("gy") * inner_y
    own = lax.dynamic_slice(extended, (jnp.int32(0), start_x, start_y), (levels, rows, columns))
    return own.transpose(1, 2, 0)


def coarse_term(residual, counts, across, along, vertical):
    piece = restrict(residual[0] / counts, across, along, vertical)
    local = coarse_whole(piece)
    return prolong(local, across, along, vertical)[None]


def provisional_state(flow_state, mass, counts, canopy, derivative):
    speed = jnp.sqrt(
        flow_state[0] * flow_state[0]
        + flow_state[1] * flow_state[1]
        + flow_state[2] * flow_state[2]
    )
    drag = drag_strength * canopy * speed
    forcing = jnp.stack(
        [
            -drag * flow_state[0],
            -drag * flow_state[1],
            -drag * flow_state[2] + buoyancy * flow_state[3],
            heating * canopy,
        ]
    )
    advection = -(
        flow_state[0] * along_x(flow_state, derivative)
        + flow_state[1] * along_y(flow_state, derivative)
        + flow_state[2] * along_z(flow_state, derivative)
    )
    rate = mass * (advection + forcing) - viscosity * stiffness_action(flow_state, mass, derivative)
    updated = flow_state + time_step * assemble(rate) / (mass * counts)
    height = flow_state.shape[3]
    vertical_index = jnp.arange(height, dtype=jnp.int32)
    wall = jnp.where((vertical_index == 0) | (vertical_index == height - 1), 0.0, 1.0).astype(
        jnp.float32
    )
    return jnp.concatenate([updated[:2], updated[2:3] * wall, updated[3:]], axis=0)


def pressure_source(provisional, mass, derivative):
    divergence = (
        along_x(provisional[0:1], derivative)
        + along_y(provisional[1:2], derivative)
        + along_z(provisional[2:3], derivative)
    )
    return -assemble(mass * divergence)


def corrected_state(provisional, pressure, mass, counts, derivative):
    gradient = jnp.concatenate(
        [
            along_x(pressure, derivative),
            along_y(pressure, derivative),
            along_z(pressure, derivative),
        ],
        axis=0,
    )
    velocity = provisional[:3] - assemble(mass * gradient) / (mass * counts)
    return jnp.concatenate([velocity, provisional[3:]], axis=0)


def paired_sums(residual, smoothed, image, counts):
    return lax.psum(
        (jnp.sum(residual * smoothed / counts), jnp.sum(image * smoothed / counts)), ("gx", "gy")
    )


def on_device(flow_state, building_height, pressure_old):
    gll_nodes, weights, derivative, eigen_basis, eigen_values = tables()
    first, width, depth, height = flow_state.shape
    mass = weight_grid(weights, width, depth, height)
    counts = multiplicity(width, depth, height)
    canopy = canopy_mask(building_height, height)
    across = interpolation(width, gll_nodes)
    along = interpolation(depth, gll_nodes)
    vertical = interpolation(height, gll_nodes)
    provisional = provisional_state(flow_state, mass, counts, canopy, derivative)
    source = pressure_source(provisional, mass, derivative)

    def operate(field):
        return assemble(stiffness_action(field, mass, derivative) + helmholtz_shift * mass * field)

    pressure = pressure_old[None]
    residual = source - operate(pressure)
    gamma_old = None
    alpha_old = None
    direction = None
    along_image = None
    for turn in range(ITERS):
        local = assemble(local_solve(residual, eigen_basis, eigen_values))
        smoothed = local + coarse_term(residual, counts, across, along, vertical)
        image = operate(smoothed)
        gamma, delta = paired_sums(residual, smoothed, image, counts)
        if turn == 0:
            alpha = gamma / delta
            direction = smoothed
            along_image = image
        else:
            ratio = gamma / gamma_old
            alpha = gamma / (delta - ratio * gamma / alpha_old)
            direction = smoothed + ratio * direction
            along_image = image + ratio * along_image
        pressure = pressure + alpha * direction
        if turn + 1 < ITERS:
            residual = residual - alpha * along_image
        gamma_old = gamma
        alpha_old = alpha
    new_state = corrected_state(provisional, pressure, mass, counts, derivative)
    return (new_state, pressure[0])


def solution(mesh):
    in_specs = (P(None, "gx", "gy", None), P("gx", "gy"), P("gx", "gy", None))
    out_specs = (P(None, "gx", "gy", None), P("gx", "gy", None))
    return jax.shard_map(
        on_device, mesh=mesh, in_specs=in_specs, out_specs=out_specs, check_vma=False
    )
```

profile of v0, /device:TPU:0, one launch (start us, length us, event | category | flops | bytes accessed | tf_op | source)
XLA Modules:
  0.0 306.9 jit_solution(7336507918853336555)
XLA Ops:
  3.5 1.5 broadcast_multiply_fusion
  7.5 3.0 collective-permute-start.8
  10.5 2.0 collective-permute-start.9
  14.9 1.1 reshape.1958
  18.8 0.8 copy-done.9
  25.4 1.3 fusion.2
  27.4 3.8 %collective-permute-start.1 = (f32[4,1,8,128]{3,1,2,0:T(1,128)}, f32[4,1,8,128]{3,1,2,0:T(1,128)}, u32[]{:S(2)}, u32[]{:S(2)}) collective-permute-start(f32[4,1,8,128]{3,1,2,0:T(1,128)} %get-tuple-element.102), channel_id=1, source_target_pairs={{8,0},{16,8},{24,16},{0,24},{9,1},{17,9},{25,17},{1,25},{10,2},{18... | collective-permute-start | bytes 49160 | tf_op jit(solution)/shard_map/ppermute | solution.py:42
  36.7 1.3 pad_maximum_fusion.33
  38.0 2.6 collective-permute-start.11
  45.7 0.8 fusion.205
  47.4 2.6 collective-permute-start.3
  50.0 1.6 collective-permute-done.2
  52.5 0.9 fusion.77
  54.2 0.9 slice-done
  57.4 3.8 %collective-permute-start.5 = (f32[1,1,8,128]{3,1,2,0:T(1,128)S(1)}, f32[1,1,8,128]{3,1,2,0:T(1,128)S(1)}, u32[]{:S(2)}, u32[]{:S(2)}) collective-permute-start(f32[1,1,8,128]{3,1,2,0:T(1,128)S(1)} %get-tuple-element.183), channel_id=1, source_target_pairs={{8,0},{16,8},{24,16},{0,24},{9,1},{17,9},{25,17},{1,25},{10,2},{18... | collective-permute-start | bytes 12296 | tf_op jit(solution)/shard_map/ppermute | solution.py:42
  61.3 1.6 collective-permute-done.4
  62.9 2.6 collective-permute-start.7
  65.5 1.3 collective-permute-done.6
  69.9 39.3 %all-gather = f32[32,1,68]{2,1,0:T(1,128)S(1)} all-gather(f32[1,1,68]{2,1,0:T(1,128)S(1)} %reshape.1947), channel_id=1, replica_groups=mesh['gx'=4,'gy'=8] {'gx','gy'}, dimensions={0}, use_global_device_ids=true | all-gather | bytes 8976 | tf_op jit(solution)/shard_map/all_gather | solution.py:264
  113.1 3.8 %collective-permute-start.13 = (f32[1,1,8,128]{3,2,1,0:T(8,128)S(1)}, f32[1,1,8,128]{3,2,1,0:T(8,128)S(1)}, u32[]{:S(2)}, u32[]{:S(2)}) collective-permute-start(f32[1,1,8,128]{3,2,1,0:T(8,128)S(1)} %get-tuple-element.175), channel_id=1, source_target_pairs={{8,0},{16,8},{24,16},{0,24},{9,1},{17,9},{25,17},{1,25},{10,2},{18... | collective-permute-start | bytes 12296 | tf_op jit(solution)/shard_map/ppermute | solution.py:42
  119.5 2.6 collective-permute-start.15
  122.3 1.1 collective-permute-done.14
  124.1 0.8 slice-done.3
  127.5 3.8 %collective-permute-start.17 = (f32[1,1,8,128]{3,1,2,0:T(1,128)S(1)}, f32[1,1,8,128]{3,1,2,0:T(1,128)S(1)}, u32[]{:S(2)}, u32[]{:S(2)}) collective-permute-start(f32[1,1,8,128]{3,1,2,0:T(1,128)S(1)} %get-tuple-element.171), channel_id=1, source_target_pairs={{8,0},{16,8},{24,16},{0,24},{9,1},{17,9},{25,17},{1,25},{10,2},{18... | collective-permute-start | bytes 12296 | tf_op jit(solution)/shard_map/ppermute | solution.py:42
  131.4 1.6 collective-permute-done.16
  133.0 2.6 collective-permute-start.19
  135.6 1.3 collective-permute-done.18
  137.3 0.9 fusion.126
  138.3 39.5 %all-reduce.1 = (f32[]{:T(128)}, f32[]{:T(128)}) all-reduce(f32[]{:T(128)} %get-tuple-element.81, f32[]{:T(128)} %get-tuple-element.80), channel_id=1, replica_groups=mesh['gx'=4,'gy'=8] {'gx','gy'}, use_global_device_ids=true, to_apply=%region_1.2 | all-reduce | flops 2 | bytes 16 | tf_op jit(solution)/shard_map/psum | solution.py:345
  179.9 40.7 %all-gather.1 = f32[32,1,68]{2,1,0:T(1,128)S(1)} all-gather(f32[1,1,68]{2,1,0:T(1,128)S(1)} %reshape.1949), channel_id=1, replica_groups=mesh['gx'=4,'gy'=8] {'gx','gy'}, dimensions={0}, use_global_device_ids=true | all-gather | bytes 8976 | tf_op jit(solution)/shard_map/all_gather | solution.py:264
  222.7 3.8 %collective-permute-start.21 = (f32[1,1,8,128]{3,2,1,0:T(8,128)S(1)}, f32[1,1,8,128]{3,2,1,0:T(8,128)S(1)}, u32[]{:S(2)}, u32[]{:S(2)}) collective-permute-start(f32[1,1,8,128]{3,2,1,0:T(8,128)S(1)} %get-tuple-element.167), channel_id=1, source_target_pairs={{8,0},{16,8},{24,16},{0,24},{9,1},{17,9},{25,17},{1,25},{10,2},{18... | collective-permute-start | bytes 12296 | tf_op jit(solution)/shard_map/ppermute | solution.py:42
  228.3 2.6 collective-permute-start.23
  231.2 1.1 collective-permute-done.22
  233.0 0.8 slice-done.4
  234.2 0.8 fusion.127
  236.4 3.8 %collective-permute-start.25 = (f32[1,1,8,128]{3,1,2,0:T(1,128)S(1)}, f32[1,1,8,128]{3,1,2,0:T(1,128)S(1)}, u32[]{:S(2)}, u32[]{:S(2)}) collective-permute-start(f32[1,1,8,128]{3,1,2,0:T(1,128)S(1)} %get-tuple-element.163), channel_id=1, source_target_pairs={{8,0},{16,8},{24,16},{0,24},{9,1},{17,9},{25,17},{1,25},{10,2},{18... | collective-permute-start | bytes 12296 | tf_op jit(solution)/shard_map/ppermute | solution.py:42
  240.2 1.6 collective-permute-done.24
  241.9 2.6 collective-permute-start.27
  244.5 1.3 collective-permute-done.26
  246.2 0.9 fusion.37
  247.2 39.6 %all-reduce = (f32[]{:T(128)}, f32[]{:T(128)}) all-reduce(f32[]{:T(128)} %get-tuple-element.223, f32[]{:T(128)} %fusion.37), channel_id=1, replica_groups=mesh['gx'=4,'gy'=8] {'gx','gy'}, use_global_device_ids=true, to_apply=%region_5.6 | all-reduce | flops 2 | bytes 16 | tf_op jit(solution)/shard_map/psum | solution.py:345
  293.3 2.0 collective-permute-start.28
  295.3 1.9 collective-permute-start.29
  297.2 1.7 collective-permute-done.28
  299.1 2.6 collective-permute-start.31
  301.7 1.5 collective-permute-done.30
  304.2 0.9 slice-done.1
  305.1 0.8 slice-done.2
  (435 shorter events, 55.6 us)
Async XLA Ops:
  0.6 1.1 copy-start.10
  6.7 7.0 %copy-start.1 = (f32[4,8,8,128]{3,2,1,0:T(8,128)S(1)}, f32[4,8,8,128]{3,2,1,0:T(8,128)}, u32[]{:S(2)}) copy-start(f32[4,8,8,128]{3,2,1,0:T(8,128)} %param.20) | copy-start | bytes 393220
  6.9 6.7 %copy-start.12 = (f32[1,8,8,128]{3,1,2,0:T(8,128)}, f32[1,8,8,128]{3,1,2,0:T(8,128)S(1)}, u32[]{:S(2)}) copy-start(f32[1,8,8,128]{3,1,2,0:T(8,128)S(1)} %fusion.14) | copy-start | bytes 98308
  7.5 6.1 %copy-start.30 = (f32[8,8,1,1]{1,0,3,2:T(8,128)S(1)}, f32[8,8,1,1]{1,0,3,2:T(8,128)}, u32[]{:S(2)}) copy-start(f32[8,8,1,1]{1,0,3,2:T(8,128)} %constant.380) | copy-start | bytes 772
  7.5 29.1 %collective-permute-start.8 = (f32[1,1,8,128]{3,1,2,0:T(1,128)}, f32[1,1,8,128]{3,1,2,0:T(1,128)}, u32[]{:S(2)}, u32[]{:S(2)}) collective-permute-start(f32[1,1,8,128]{3,1,2,0:T(1,128)} %get-tuple-element.178), channel_id=1, source_target_pairs={{0,8},{8,16},{16,24},{24,0},{1,9},{9,17},{17,25},{25,1},{2,10},{10... | collective-permute-start | bytes 12296 | tf_op jit(solution)/shard_map/ppermute | solution.py:40
  10.5 26.1 %collective-permute-start.9 = (f32[1,1,8,128]{3,1,2,0:T(1,128)}, f32[1,1,8,128]{3,1,2,0:T(1,128)}, u32[]{:S(2)}, u32[]{:S(2)}) collective-permute-start(f32[1,1,8,128]{3,1,2,0:T(1,128)} %get-tuple-element.179), channel_id=1, source_target_pairs={{8,0},{16,8},{24,16},{0,24},{9,1},{17,9},{25,17},{1,25},{10,2},{18... | collective-permute-start | bytes 12296 | tf_op jit(solution)/shard_map/ppermute | solution.py:42
  14.2 10.1 %copy-start.2 = (f32[8,4,8,128]{3,0,2,1:T(8,128)}, f32[8,4,8,128]{3,0,2,1:T(8,128)S(1)}, u32[]{:S(2)}) copy-start(f32[8,4,8,128]{3,0,2,1:T(8,128)S(1)} %fusion.345) | copy-start | bytes 393220
  17.3 1.3 copy-start.32
  18.7 5.6 %copy-start.3 = (f32[8,8,128]{2,0,1:T(8,128)}, f32[8,8,128]{2,0,1:T(8,128)S(1)}, u32[]{:S(2)}) copy-start(f32[8,8,128]{2,0,1:T(8,128)S(1)} %get-tuple-element.219) | copy-start | bytes 98308
  24.3 1.0 copy-start.17
  24.3 1.0 copy-start.21
  24.3 1.0 copy-start.25
  24.3 0.9 copy-start.26
  25.4 18.5 %copy-start = (f32[16,8,16,8]{3,2,1,0:T(8,128)S(1)}, f32[16,8,16,8]{3,2,1,0:T(8,128)}, u32[]{:S(2)}) copy-start(f32[16,8,16,8]{3,2,1,0:T(8,128)} %get-tuple-element.210) | copy-start | bytes 196612
  26.7 9.9 %copy-start.13 = (f32[1,8,8,128]{3,1,2,0:T(8,128)S(1)}, f32[1,8,8,128]{3,1,2,0:T(8,128)}, u32[]{:S(2)}) copy-start(f32[1,8,8,128]{3,1,2,0:T(8,128)} %copy-done.12) | copy-start | bytes 98308
  27.4 19.2 %collective-permute-start = (f32[4,1,8,128]{3,1,2,0:T(1,128)}, f32[4,1,8,128]{3,1,2,0:T(1,128)S(1)}, u32[]{:S(2)}, u32[]{:S(2)}) collective-permute-start(f32[4,1,8,128]{3,1,2,0:T(1,128)} %get-tuple-element.101), channel_id=1, source_target_pairs={{0,8},{8,16},{16,24},{24,0},{1,9},{9,17},{17,25},{25,1},{2,10},{10... | collective-permute-start | bytes 49160 | tf_op jit(solution)/shard_map/ppermute | solution.py:40
  27.4 19.2 %collective-permute-start.1 = (f32[4,1,8,128]{3,1,2,0:T(1,128)}, f32[4,1,8,128]{3,1,2,0:T(1,128)}, u32[]{:S(2)}, u32[]{:S(2)}) collective-permute-start(f32[4,1,8,128]{3,1,2,0:T(1,128)} %get-tuple-element.102), channel_id=1, source_target_pairs={{8,0},{16,8},{24,16},{0,24},{9,1},{17,9},{25,17},{1,25},{10,2},{18... | collective-permute-start | bytes 49160 | tf_op jit(solution)/shard_map/ppermute | solution.py:42
  38.0 7.0 %collective-permute-start.10 = (f32[1,10,1,128]{3,1,2,0:T(8,128)}, f32[1,10,1,128]{3,1,2,0:T(8,128)S(1)}, u32[]{:S(2)}, u32[]{:S(2)}) collective-permute-start(f32[1,10,1,128]{3,1,2,0:T(8,128)} %get-tuple-element.150), channel_id=1, source_target_pairs={{0,1},{1,2},{2,3},{3,4},{4,5},{5,6},{6,7},{7,0},{8,9},{9,10},{10,1... | collective-permute-start | bytes 15368 | tf_op jit(solution)/shard_map/ppermute | solution.py:40
  38.0 7.0 %collective-permute-start.11 = (f32[1,10,1,128]{3,1,2,0:T(8,128)}, f32[1,10,1,128]{3,1,2,0:T(8,128)S(1)}, u32[]{:S(2)}, u32[]{:S(2)}) collective-permute-start(f32[1,10,1,128]{3,1,2,0:T(8,128)} %get-tuple-element.151), channel_id=1, source_target_pairs={{1,0},{2,1},{3,2},{4,3},{5,4},{6,5},{7,6},{0,7},{9,8},{10,9},{11,1... | collective-permute-start | bytes 15368 | tf_op jit(solution)/shard_map/ppermute | solution.py:42
  41.7 2.2 copy-start.28
  47.3 4.3 %collective-permute-start.2 = (f32[4,10,1,128]{3,1,2,0:T(8,128)S(1)}, f32[4,10,1,128]{3,1,2,0:T(8,128)S(1)}, u32[]{:S(2)}, u32[]{:S(2)}) collective-permute-start(f32[4,10,1,128]{3,1,2,0:T(8,128)S(1)} %get-tuple-element.92), channel_id=1, source_target_pairs={{0,1},{1,2},{2,3},{3,4},{4,5},{5,6},{6,7},{7,0},{8,9},{9,10},{10,1... | collective-permute-start | bytes 61448 | tf_op jit(solution)/shard_map/ppermute | solution.py:40
  47.4 4.2 %collective-permute-start.3 = (f32[4,10,1,128]{3,1,2,0:T(8,128)S(1)}, f32[4,10,1,128]{3,1,2,0:T(8,128)S(1)}, u32[]{:S(2)}, u32[]{:S(2)}) collective-permute-start(f32[4,10,1,128]{3,1,2,0:T(8,128)S(1)} %get-tuple-element.93), channel_id=1, source_target_pairs={{1,0},{2,1},{3,2},{4,3},{5,4},{6,5},{7,6},{0,7},{9,8},{10,9},{11,1... | collective-permute-start | bytes 61448 | tf_op jit(solution)/shard_map/ppermute | solution.py:42
  56.1 245.6 %copy-start.20 = (f32[4,8,8,128]{3,2,1,0:T(8,128)}, f32[4,8,8,128]{3,2,1,0:T(8,128)S(1)}, u32[]{:S(2)}) copy-start(f32[4,8,8,128]{3,2,1,0:T(8,128)S(1)} %fusion.4) | copy-start | bytes 393220
  57.4 5.5 %collective-permute-start.4 = (f32[1,1,8,128]{3,1,2,0:T(1,128)S(1)}, f32[1,1,8,128]{3,1,2,0:T(1,128)S(1)}, u32[]{:S(2)}, u32[]{:S(2)}) collective-permute-start(f32[1,1,8,128]{3,1,2,0:T(1,128)S(1)} %get-tuple-element.182), channel_id=1, source_target_pairs={{0,8},{8,16},{16,24},{24,0},{1,9},{9,17},{17,25},{25,1},{2,10},{10... | collective-permute-start | bytes 12296 | tf_op jit(solution)/shard_map/ppermute | solution.py:40
  57.4 5.4 %collective-permute-start.5 = (f32[1,1,8,128]{3,1,2,0:T(1,128)S(1)}, f32[1,1,8,128]{3,1,2,0:T(1,128)S(1)}, u32[]{:S(2)}, u32[]{:S(2)}) collective-permute-start(f32[1,1,8,128]{3,1,2,0:T(1,128)S(1)} %get-tuple-element.183), channel_id=1, source_target_pairs={{8,0},{16,8},{24,16},{0,24},{9,1},{17,9},{25,17},{1,25},{10,2},{18... | collective-permute-start | bytes 12296 | tf_op jit(solution)/shard_map/ppermute | solution.py:42
  62.8 4.0 %collective-permute-start.6 = (f32[1,10,1,128]{3,1,2,0:T(8,128)S(1)}, f32[1,10,1,128]{3,1,2,0:T(8,128)S(1)}, u32[]{:S(2)}, u32[]{:S(2)}) collective-permute-start(f32[1,10,1,128]{3,1,2,0:T(8,128)S(1)} %get-tuple-element.156), channel_id=1, source_target_pairs={{0,1},{1,2},{2,3},{3,4},{4,5},{5,6},{6,7},{7,0},{8,9},{9,10},{10,1... | collective-permute-start | bytes 15368 | tf_op jit(solution)/shard_map/ppermute | solution.py:40
  62.9 4.0 %collective-permute-start.7 = (f32[1,10,1,128]{3,1,2,0:T(8,128)S(1)}, f32[1,10,1,128]{3,1,2,0:T(8,128)S(1)}, u32[]{:S(2)}, u32[]{:S(2)}) collective-permute-start(f32[1,10,1,128]{3,1,2,0:T(8,128)S(1)} %get-tuple-element.157), channel_id=1, source_target_pairs={{1,0},{2,1},{3,2},{4,3},{5,4},{6,5},{7,6},{0,7},{9,8},{10,9},{11,1... | collective-permute-start | bytes 15368 | tf_op jit(solution)/shard_map/ppermute | solution.py:42
  113.0 6.3 %collective-permute-start.12 = (f32[1,1,8,128]{3,2,1,0:T(8,128)S(1)}, f32[1,1,8,128]{3,2,1,0:T(8,128)S(1)}, u32[]{:S(2)}, u32[]{:S(2)}) collective-permute-start(f32[1,1,8,128]{3,2,1,0:T(8,128)S(1)} %get-tuple-element.174), channel_id=1, source_target_pairs={{0,8},{8,16},{16,24},{24,0},{1,9},{9,17},{17,25},{25,1},{2,10},{10... | collective-permute-start | bytes 12296 | tf_op jit(solution)/shard_map/ppermute | solution.py:40
  113.1 6.3 %collective-permute-start.13 = (f32[1,1,8,128]{3,2,1,0:T(8,128)S(1)}, f32[1,1,8,128]{3,2,1,0:T(8,128)S(1)}, u32[]{:S(2)}, u32[]{:S(2)}) collective-permute-start(f32[1,1,8,128]{3,2,1,0:T(8,128)S(1)} %get-tuple-element.175), channel_id=1, source_target_pairs={{8,0},{16,8},{24,16},{0,24},{9,1},{17,9},{25,17},{1,25},{10,2},{18... | collective-permute-start | bytes 12296 | tf_op jit(solution)/shard_map/ppermute | solution.py:42
  119.4 4.0 %collective-permute-start.14 = (f32[1,10,1,128]{3,2,1,0:T(1,128)S(1)}, f32[1,10,1,128]{3,2,1,0:T(1,128)S(1)}, u32[]{:S(2)}, u32[]{:S(2)}) collective-permute-start(f32[1,10,1,128]{3,2,1,0:T(1,128)S(1)} %get-tuple-element.144), channel_id=1, source_target_pairs={{0,1},{1,2},{2,3},{3,4},{4,5},{5,6},{6,7},{7,0},{8,9},{9,10},{10,1... | collective-permute-start | bytes 15368 | tf_op jit(solution)/shard_map/ppermute | solution.py:40
  119.5 4.0 %collective-permute-start.15 = (f32[1,10,1,128]{3,2,1,0:T(1,128)S(1)}, f32[1,10,1,128]{3,2,1,0:T(1,128)S(1)}, u32[]{:S(2)}, u32[]{:S(2)}) collective-permute-start(f32[1,10,1,128]{3,2,1,0:T(1,128)S(1)} %get-tuple-element.145), channel_id=1, source_target_pairs={{1,0},{2,1},{3,2},{4,3},{5,4},{6,5},{7,6},{0,7},{9,8},{10,9},{11,1... | collective-permute-start | bytes 15368 | tf_op jit(solution)/shard_map/ppermute | solution.py:42
  127.5 5.5 %collective-permute-start.16 = (f32[1,1,8,128]{3,1,2,0:T(1,128)S(1)}, f32[1,1,8,128]{3,1,2,0:T(1,128)S(1)}, u32[]{:S(2)}, u32[]{:S(2)}) collective-permute-start(f32[1,1,8,128]{3,1,2,0:T(1,128)S(1)} %get-tuple-element.170), channel_id=1, source_target_pairs={{0,8},{8,16},{16,24},{24,0},{1,9},{9,17},{17,25},{25,1},{2,10},{10... | collective-permute-start | bytes 12296 | tf_op jit(solution)/shard_map/ppermute | solution.py:40
  127.5 5.4 %collective-permute-start.17 = (f32[1,1,8,128]{3,1,2,0:T(1,128)S(1)}, f32[1,1,8,128]{3,1,2,0:T(1,128)S(1)}, u32[]{:S(2)}, u32[]{:S(2)}) collective-permute-start(f32[1,1,8,128]{3,1,2,0:T(1,128)S(1)} %get-tuple-element.171), channel_id=1, source_target_pairs={{8,0},{16,8},{24,16},{0,24},{9,1},{17,9},{25,17},{1,25},{10,2},{18... | collective-permute-start | bytes 12296 | tf_op jit(solution)/shard_map/ppermute | solution.py:42
  133.0 4.0 %collective-permute-start.18 = (f32[1,10,1,128]{3,1,2,0:T(8,128)S(1)}, f32[1,10,1,128]{3,1,2,0:T(8,128)S(1)}, u32[]{:S(2)}, u32[]{:S(2)}) collective-permute-start(f32[1,10,1,128]{3,1,2,0:T(8,128)S(1)} %get-tuple-element.142), channel_id=1, source_target_pairs={{0,1},{1,2},{2,3},{3,4},{4,5},{5,6},{6,7},{7,0},{8,9},{9,10},{10,1... | collective-permute-start | bytes 15368 | tf_op jit(solution)/shard_map/ppermute | solution.py:40
  133.0 4.0 %collective-permute-start.19 = (f32[1,10,1,128]{3,1,2,0:T(8,128)S(1)}, f32[1,10,1,128]{3,1,2,0:T(8,128)S(1)}, u32[]{:S(2)}, u32[]{:S(2)}) collective-permute-start(f32[1,10,1,128]{3,1,2,0:T(8,128)S(1)} %get-tuple-element.143), channel_id=1, source_target_pairs={{1,0},{2,1},{3,2},{4,3},{5,4},{6,5},{7,6},{0,7},{9,8},{10,9},{11,1... | collective-permute-start | bytes 15368 | tf_op jit(solution)/shard_map/ppermute | solution.py:42
  222.6 5.6 %collective-permute-start.20 = (f32[1,1,8,128]{3,2,1,0:T(8,128)S(1)}, f32[1,1,8,128]{3,2,1,0:T(8,128)S(1)}, u32[]{:S(2)}, u32[]{:S(2)}) collective-permute-start(f32[1,1,8,128]{3,2,1,0:T(8,128)S(1)} %get-tuple-element.166), channel_id=1, source_target_pairs={{0,8},{8,16},{16,24},{24,0},{1,9},{9,17},{17,25},{25,1},{2,10},{10... | collective-permute-start | bytes 12296 | tf_op jit(solution)/shard_map/ppermute | solution.py:40
  222.7 5.6 %collective-permute-start.21 = (f32[1,1,8,128]{3,2,1,0:T(8,128)S(1)}, f32[1,1,8,128]{3,2,1,0:T(8,128)S(1)}, u32[]{:S(2)}, u32[]{:S(2)}) collective-permute-start(f32[1,1,8,128]{3,2,1,0:T(8,128)S(1)} %get-tuple-element.167), channel_id=1, source_target_pairs={{8,0},{16,8},{24,16},{0,24},{9,1},{17,9},{25,17},{1,25},{10,2},{18... | collective-permute-start | bytes 12296 | tf_op jit(solution)/shard_map/ppermute | solution.py:42
  228.3 4.0 %collective-permute-start.22 = (f32[1,10,1,128]{3,2,1,0:T(1,128)S(1)}, f32[1,10,1,128]{3,2,1,0:T(1,128)S(1)}, u32[]{:S(2)}, u32[]{:S(2)}) collective-permute-start(f32[1,10,1,128]{3,2,1,0:T(1,128)S(1)} %get-tuple-element.136), channel_id=1, source_target_pairs={{0,1},{1,2},{2,3},{3,4},{4,5},{5,6},{6,7},{7,0},{8,9},{9,10},{10,1... | collective-permute-start | bytes 15368 | tf_op jit(solution)/shard_map/ppermute | solution.py:40
  228.3 4.0 %collective-permute-start.23 = (f32[1,10,1,128]{3,2,1,0:T(1,128)S(1)}, f32[1,10,1,128]{3,2,1,0:T(1,128)S(1)}, u32[]{:S(2)}, u32[]{:S(2)}) collective-permute-start(f32[1,10,1,128]{3,2,1,0:T(1,128)S(1)} %get-tuple-element.137), channel_id=1, source_target_pairs={{1,0},{2,1},{3,2},{4,3},{5,4},{6,5},{7,6},{0,7},{9,8},{10,9},{11,1... | collective-permute-start | bytes 15368 | tf_op jit(solution)/shard_map/ppermute | solution.py:42
  236.3 5.5 %collective-permute-start.24 = (f32[1,1,8,128]{3,1,2,0:T(1,128)S(1)}, f32[1,1,8,128]{3,1,2,0:T(1,128)S(1)}, u32[]{:S(2)}, u32[]{:S(2)}) collective-permute-start(f32[1,1,8,128]{3,1,2,0:T(1,128)S(1)} %get-tuple-element.162), channel_id=1, source_target_pairs={{0,8},{8,16},{16,24},{24,0},{1,9},{9,17},{17,25},{25,1},{2,10},{10... | collective-permute-start | bytes 12296 | tf_op jit(solution)/shard_map/ppermute | solution.py:40
  236.4 5.4 %collective-permute-start.25 = (f32[1,1,8,128]{3,1,2,0:T(1,128)S(1)}, f32[1,1,8,128]{3,1,2,0:T(1,128)S(1)}, u32[]{:S(2)}, u32[]{:S(2)}) collective-permute-start(f32[1,1,8,128]{3,1,2,0:T(1,128)S(1)} %get-tuple-element.163), channel_id=1, source_target_pairs={{8,0},{16,8},{24,16},{0,24},{9,1},{17,9},{25,17},{1,25},{10,2},{18... | collective-permute-start | bytes 12296 | tf_op jit(solution)/shard_map/ppermute | solution.py:42
  241.8 4.0 %collective-permute-start.26 = (f32[1,10,1,128]{3,1,2,0:T(8,128)S(1)}, f32[1,10,1,128]{3,1,2,0:T(8,128)S(1)}, u32[]{:S(2)}, u32[]{:S(2)}) collective-permute-start(f32[1,10,1,128]{3,1,2,0:T(8,128)S(1)} %get-tuple-element.134), channel_id=1, source_target_pairs={{0,1},{1,2},{2,3},{3,4},{4,5},{5,6},{6,7},{7,0},{8,9},{9,10},{10,1... | collective-permute-start | bytes 15368 | tf_op jit(solution)/shard_map/ppermute | solution.py:40
  241.9 4.0 %collective-permute-start.27 = (f32[1,10,1,128]{3,1,2,0:T(8,128)S(1)}, f32[1,10,1,128]{3,1,2,0:T(8,128)S(1)}, u32[]{:S(2)}, u32[]{:S(2)}) collective-permute-start(f32[1,10,1,128]{3,1,2,0:T(8,128)S(1)} %get-tuple-element.135), channel_id=1, source_target_pairs={{1,0},{2,1},{3,2},{4,3},{5,4},{6,5},{7,6},{0,7},{9,8},{10,9},{11,1... | collective-permute-start | bytes 15368 | tf_op jit(solution)/shard_map/ppermute | solution.py:42
  246.2 45.2 %copy-start.11 = (f32[8,8,128]{2,1,0:T(8,128)S(1)}, f32[8,8,128]{2,1,0:T(8,128)}, u32[]{:S(2)}) copy-start(f32[8,8,128]{2,1,0:T(8,128)} %param.22) | copy-start | bytes 98308
  293.3 5.5 %collective-permute-start.28 = (f32[3,1,8,128]{3,1,2,0:T(1,128)S(1)}, f32[3,1,8,128]{3,1,2,0:T(1,128)S(1)}, u32[]{:S(2)}, u32[]{:S(2)}) collective-permute-start(f32[3,1,8,128]{3,1,2,0:T(1,128)S(1)} %get-tuple-element.114), channel_id=1, source_target_pairs={{0,8},{8,16},{16,24},{24,0},{1,9},{9,17},{17,25},{25,1},{2,10},{10... | collective-permute-start | bytes 36872 | tf_op jit(solution)/shard_map/ppermute | solution.py:40
  295.3 3.7 %collective-permute-start.29 = (f32[3,1,8,128]{3,1,2,0:T(1,128)S(1)}, f32[3,1,8,128]{3,1,2,0:T(1,128)S(1)}, u32[]{:S(2)}, u32[]{:S(2)}) collective-permute-start(f32[3,1,8,128]{3,1,2,0:T(1,128)S(1)} %get-tuple-element.115), channel_id=1, source_target_pairs={{8,0},{16,8},{24,16},{0,24},{9,1},{17,9},{25,17},{1,25},{10,2},{18... | collective-permute-start | bytes 36872 | tf_op jit(solution)/shard_map/ppermute | solution.py:42
  299.0 4.2 %collective-permute-start.30 = (f32[3,10,1,128]{3,1,2,0:T(8,128)S(1)}, f32[3,10,1,128]{3,1,2,0:T(8,128)S(1)}, u32[]{:S(2)}, u32[]{:S(2)}) collective-permute-start(f32[3,10,1,128]{3,1,2,0:T(8,128)S(1)} %get-tuple-element.110), channel_id=1, source_target_pairs={{0,1},{1,2},{2,3},{3,4},{4,5},{5,6},{6,7},{7,0},{8,9},{9,10},{10,1... | collective-permute-start | bytes 46088 | tf_op jit(solution)/shard_map/ppermute | solution.py:40
  299.1 4.2 %collective-permute-start.31 = (f32[3,10,1,128]{3,1,2,0:T(8,128)S(1)}, f32[3,10,1,128]{3,1,2,0:T(8,128)S(1)}, u32[]{:S(2)}, u32[]{:S(2)}) collective-permute-start(f32[3,10,1,128]{3,1,2,0:T(8,128)S(1)} %get-tuple-element.111), channel_id=1, source_target_pairs={{1,0},{2,1},{3,2},{4,3},{5,4},{6,5},{7,6},{0,7},{9,8},{10,9},{11,1... | collective-permute-start | bytes 46088 | tf_op jit(solution)/shard_map/ppermute | solution.py:42
  (50 other events, 35.4 us)
where the time goes:
time: 310 us; the launch traced here: 307 us
  blocking collectives  159 us (51%)
  starting transfers between devices  53.6 us (17%)
  local copies, waits for them, and re-layouts  30.6 us (10%)
  matrix products  19.6 us (6%)
  other arithmetic  18.8 us (6%)
  waiting for transfers between devices  16.1 us (5%)
  between operations  9.26 us (3%)
    all_gather x2, blocking collectives, coarse_whole(): lax.all_gather(piece.reshape(1, rows * columns * levels), ('gx', 'gy'), a...  80 us
    psum x2, blocking collectives, paired_sums(): lax.psum((jnp.sum(residual * smoothed / counts), jnp.sum(image * smoothed...  79.1 us
    ppermute x16, starting transfers between devices, padded_2(): lax.ppermute(head, axis, [((i + 1) % count, i) for i in range(count)])  47.8 us
    unnamed x138, local copies, waits for them, and re-layouts  16.5 us
    ppermute x16, waiting for transfers between devices, padded_2(): lax.ppermute(tail, axis, [(i, (i + 1) % count) for i in range(count)])  15.7 us
  transfers between devices with their start and end apart: 32, of which 12 were waited for; matrix products, arithmetic and copies ran while one was open for 8% of the time, Pallas kernels for 0%

commit v1 on v0

v1 whole, which is shorter than its diff:
```python
import functools
import math

import jax
import jax.numpy as jnp
import ml_dtypes
import numpy as np
from jax import lax
from jax.experimental import pallas as pl
from jax.experimental.pallas import tpu as pltpu
from jax.sharding import PartitionSpec as P

F32 = jnp.float32
BF16 = jnp.bfloat16
MESH = pl.DeviceIdType.MESH
N = 8
viscosity = 0.05
time_step = 0.01
drag_strength = 20.0
heating = 40.0
buoyancy = 10.0
helmholtz_shift = 0.001
local_shift = 0.5
coarse_shift = 0.02
gll_points = (
    -1.0,
    -0.8717401485096066,
    -0.5917001814331423,
    -0.2092992179024789,
    0.2092992179024789,
    0.5917001814331423,
    0.8717401485096066,
    1.0,
)


def legendre_seven(points):
    squared = points * points
    return points * (((429.0 * squared - 693.0) * squared + 315.0) * squared - 35.0) / 16.0


def jacobi_eigen(matrix):
    current = np.array(matrix)
    basis = np.eye(8)
    for rounds in range(12):
        for first in range(7):
            for second in range(first + 1, 8):
                rotation_angle = 0.5 * math.atan2(
                    2.0 * float(current[first, second]),
                    float(current[second, second] - current[first, first]),
                )
                cosine = math.cos(rotation_angle)
                sine = math.sin(rotation_angle)
                rotation = np.eye(8)
                rotation[first, first] = cosine
                rotation[second, second] = cosine
                rotation[first, second] = sine
                rotation[second, first] = -sine
                current = rotation.T @ current @ rotation
                basis = basis @ rotation
    return (np.sum(current * np.eye(8), axis=0), basis)


def gll_tables():
    gll_nodes = np.array(gll_points)
    values = legendre_seven(gll_nodes)
    weights = 2.0 / (56.0 * values * values)
    differ = gll_nodes[:, None] - gll_nodes[None, :] + np.eye(8)
    derivative = values[:, None] / values[None, :] / differ * (1.0 - np.eye(8))
    derivative = (
        derivative + np.eye(8) * np.array([-14.0, 0.0, 0.0, 0.0, 0.0, 0.0, 0.0, 14.0])[None, :]
    )
    stiffness = derivative.T @ (weights[:, None] * derivative)
    scaled = stiffness / np.sqrt(np.outer(weights, weights))
    scaled = 0.5 * (scaled + scaled.T)
    eigen_values, eigen_vectors = jacobi_eigen(scaled)
    eigen_basis = eigen_vectors / np.sqrt(weights)[:, None]
    return (gll_nodes, weights, derivative, eigen_basis, np.maximum(eigen_values, 0.0))


def hartley_tables(count):
    index = np.arange(count)
    angle = 2.0 * np.pi / count * (index[:, None] * index[None, :] % count)
    hartley = (np.cos(angle) + np.sin(angle)) / np.sqrt(count)
    return hartley, 2.0 - 2.0 * np.cos(2.0 * np.pi / count * index)


def cosine_tables(count):
    index = np.arange(count)
    angle = np.pi / count * (index[:, None] + 0.5) * index[None, :]
    norms = np.where(index == 0, np.sqrt(1.0 / count), np.sqrt(2.0 / count))
    return np.cos(angle) * norms[None, :], 2.0 - 2.0 * np.cos(np.pi / count * index)


def thirds(matrix):
    pieces = []
    for piece in range(3):
        pieces.append(matrix.astype(np.float32).astype(ml_dtypes.bfloat16))
        matrix = matrix - pieces[-1].astype(np.float64)
    return pieces


def mode_pieces(modes):
    return modes // 128 if modes > 128 and modes % 128 == 0 else 1


DX, DY, KXY = range(3)
ZD, ZK, ZRESTRICT = range(3)
FORWARD, BACK = range(2)
ZFORWARD, ZBACK, ZPROLONG = range(3)
MASS, WXY, WZ, STEP, INVERSE, COPIES, SPECTRUM, CORNERS, SIDES = range(9)


@functools.lru_cache(maxsize=None)
def constants(parts_x, parts_y, height):
    nodes, weights, derivative, basis, values = gll_tables()
    layers = height // N
    levels = layers + 1
    group = height // 4
    assert levels <= group
    eye = np.eye(N)
    diagonal = np.diag(weights)
    stiffness = derivative.T @ diagonal @ derivative

    lefts = np.concatenate(
        [
            np.kron(derivative, eye),
            np.kron(eye, derivative),
            np.kron(stiffness, diagonal) + np.kron(diagonal, stiffness),
        ],
        axis=0,
    )
    high, low, rest = thirds(lefts)
    left_exact = np.concatenate([high, high, low, low, rest], axis=1)
    high, low, rest = thirds(np.concatenate([np.kron(basis.T, basis.T), np.kron(basis, basis)]))
    left_table = np.concatenate([high, high, low, low], axis=1)

    near, far = (1.0 - nodes) / 2.0, (1.0 + nodes) / 2.0
    vertical = np.zeros((height, levels))
    for layer in range(layers):
        vertical[layer * N : layer * N + N, layer] = near
        vertical[layer * N : layer * N + N, layer + 1] = far
    cosine, eigen_z = cosine_tables(levels)
    prolong_z = vertical @ cosine
    place = np.arange(height)
    face = np.where((np.arange(N) == 0) | (np.arange(N) == N - 1), 2.0, 1.0)
    count_z = np.where((place == 0) | (place == height - 1), 1.0, np.tile(face, layers))
    grouped = np.zeros((height, 4, group))
    grouped[:, :, :levels] = prolong_z[:, None, :]
    grouped = grouped.reshape(height, height)
    many = np.eye(layers)
    rights = [np.kron(many, derivative.T), np.kron(many, stiffness)]
    high, low, rest = thirds(np.concatenate(rights, axis=1))
    right_exact = np.concatenate([high, high, low, low, rest], axis=0)
    high, low, rest = thirds(grouped / count_z[:, None])
    right_exact = np.concatenate(
        [right_exact, np.concatenate([high, high, low, low, high], axis=0)], axis=1
    )
    rights = [np.kron(many, basis), np.kron(many, basis.T), grouped.T]
    high, low, rest = thirds(np.concatenate(rights, axis=1))
    right_table = np.concatenate([high, high, low], axis=0)

    weight_xy = np.kron(weights, weights)[:, None] * np.ones((1, height))
    weight_z = np.ones((N * N, 1)) * np.tile(weights, layers)[None, :]
    mass = weight_xy * weight_z
    count_xy = np.kron(face, face)
    copies = count_xy[:, None] * count_z[None, :]
    spectrum = (values[:, None] + values[None, :]).reshape(-1)[:, None] + np.tile(values, layers)
    near_x, far_x = np.repeat(near, N), np.repeat(far, N)
    near_y, far_y = np.tile(near, N), np.tile(far, N)
    sides = np.zeros((N * N, height))
    sides[:, 0], sides[:, 1], sides[:, 2], sides[:, 3] = near_x, far_x, near_y, far_y
    corner = np.stack([near_x * near_y, near_x * far_y, far_x * near_y, far_x * far_y], axis=1)
    corners = np.repeat(corner / count_xy[:, None], group, axis=1)
    plain = np.concatenate(
        [
            mass,
            weight_xy,
            weight_z,
            time_step / (mass * copies),
            1.0 / (mass * copies),
            1.0 / copies,
            1.0 / (spectrum + local_shift),
            corners,
            sides,
        ],
        axis=0,
    ).astype(np.float32)

    hartley_x, eigen_x = hartley_tables(parts_x)
    hartley_y, eigen_y = hartley_tables(parts_y)
    vertex = []
    for step_x in (0, 1):
        for step_y in (0, 1):
            vertex.append(
                np.kron(np.roll(hartley_x, -step_x, axis=1), np.roll(hartley_y, -step_y, axis=1))
            )
    modes = parts_x * parts_y
    pieces = mode_pieces(modes)
    high, low, rest = thirds(np.stack(vertex))
    vertex_table = np.stack([high, low]).reshape(8, pieces, modes // pieces, modes)
    vertex_table = vertex_table.transpose(1, 0, 2, 3).reshape(pieces, -1, modes)
    rows = np.concatenate(
        [np.repeat(hartley_x, parts_y, axis=1), np.tile(hartley_y, (1, parts_x))], axis=0
    ).astype(np.float32)
    rows = rows.reshape(parts_x + parts_y, pieces, -1).transpose(1, 0, 2)
    horizontal = (eigen_x[:, None] + eigen_y[None, :]).reshape(-1)
    inverse = np.zeros((modes, 4, group))
    inverse[:, :, :levels] = (
        1.0 / (2.0 * (horizontal[:, None] + eigen_z[None, :]) + coarse_shift)
    )[:, None, :]
    inverse = inverse.reshape(pieces, -1, height).astype(np.float32)
    return left_exact, right_exact, left_table, right_table, plain, vertex_table, rows, inverse


def split(values):
    high = values.astype(BF16)
    return high, (values - high.astype(F32)).astype(BF16)


def split_thrice(values):
    high = values.astype(BF16)
    rest = values - high.astype(F32)
    low = rest.astype(BF16)
    return high, low, (rest - low.astype(F32)).astype(BF16)


def product(first, second):
    return jnp.dot(first, second, preferred_element_type=F32)


EXCHANGES = (4, 1, 1, 1, 1, 3, 6)
GATHERS = 4


def kernel(
    parts,
    flow_ref,
    roof_ref,
    old_ref,
    left_exact_ref,
    right_exact_ref,
    left_ref,
    right_ref,
    plain_ref,
    vertex_ref,
    rows_ref,
    modes_ref,
    state_ref,
    pressure_ref,
    *scratch,
):
    parts_x, parts_y = parts
    devices = parts_x * parts_y
    count = len(EXCHANGES)
    fields = scratch[0:count]
    y_out = scratch[count : 2 * count]
    c_out = scratch[2 * count : 3 * count]
    x_in = scratch[3 * count : 4 * count]
    y_in = scratch[4 * count : 5 * count]
    c_in = scratch[5 * count : 6 * count]
    row_out, gathered, send_sem, recv_sem, row_send, row_recv = scratch[6 * count :]
    height = old_ref.shape[1]
    points = old_ref.shape[0]

    my_x, my_y = lax.axis_index("gx"), lax.axis_index("gy")
    me = my_x * parts_y + my_y

    barrier = pltpu.get_barrier_semaphore()

    def greet(step, carry):
        other = lax.rem(me + step, devices)
        pl.semaphore_signal(
            barrier, inc=1, device_id=(other // parts_y, lax.rem(other, parts_y)), device_id_type=MESH
        )
        return carry

    lax.fori_loop(1, devices, greet, 0)

    before_x, after_x = lax.rem(my_x + parts_x - 1, parts_x), lax.rem(my_x + 1, parts_x)
    before_y, after_y = lax.rem(my_y + parts_y - 1, parts_y), lax.rem(my_y + 1, parts_y)

    def block(which):
        return plain_ref[which * points : (which + 1) * points, :]

    def left_exact(values, first, last):
        high, low = split(values)
        stacked = jnp.concatenate([high, low, high, low, high], axis=0)
        return product(left_exact_ref[first * points : last * points, :], stacked)

    def right_exact(values, first, last):
        high, low = split(values)
        stacked = jnp.concatenate([high, low, high, low, high], axis=1)
        return product(stacked, right_exact_ref[:, first * height : last * height])

    def left(values, first, last):
        high, low = split(values)
        stacked = jnp.concatenate([high, low, high, low], axis=0)
        return product(left_ref[first * points : last * points, :], stacked)

    def right(values, first, last):
        high, low = split(values)
        stacked = jnp.concatenate([high, low, high], axis=1)
        return product(stacked, right_ref[:, first * height : last * height])

    lane = lax.broadcasted_iota(jnp.int32, (points, height), 1)
    joins_up = (lax.rem(lane, N) == N - 1) & (lane < height - 1)
    joins_down = (lax.rem(lane, N) == 0) & (lane > 0)

    def pair_z(values):
        up = pltpu.roll(values, height - 1, 1)
        down = pltpu.roll(values, 1, 1)
        return values + jnp.where(joins_up, up, jnp.where(joins_down, down, 0.0))

    def copies(which):
        field, number = fields[which], EXCHANGES[which]
        plan = []
        x_faces = (field.at[:, points - N : points, :], field.at[:, 0:N, :])
        for side, target in ((0, after_x), (1, before_x)):
            plan.append((x_faces[side], x_in[which].at[side], (target, my_y)))
        for side, target in ((0, after_y), (1, before_y)):
            plan.append((y_out[which].at[side], y_in[which].at[side], (my_x, target)))
        for corner, target in enumerate(
            ((after_x, after_y), (after_x, before_y), (before_x, after_y), (before_x, before_y))
        ):
            plan.append((c_out[which].at[corner], c_in[which].at[corner], target))
        return [
            pltpu.make_async_remote_copy(
                src_ref=source,
                dst_ref=landing,
                send_sem=send_sem.at[which, index],
                recv_sem=recv_sem.at[which, index],
                device_id=target,
                device_id_type=MESH,
            )
            for index, (source, landing, target) in enumerate(plan)
        ]

    def start(which, values):
        field, number = fields[which], EXCHANGES[which]
        values = [pair_z(value) for value in values]
        for index, value in enumerate(values):
            field[index] = value
            solid = value.reshape(N, N, height)
            y_out[which][0, index * N : index * N + N, :] = solid[:, N - 1, :]
            y_out[which][1, index * N : index * N + N, :] = solid[:, 0, :]
            for corner, row in enumerate((points - 1, points - N, N - 1, 0)):
                c_out[which][corner, index : index + 1, :] = value[row : row + 1, :]
        plan = copies(which)
        for copy in plan:
            copy.start()
        return values

    row_of_x = lax.broadcasted_iota(jnp.int32, (N, height), 0)

    def finish(which, values):
        plan = copies(which)
        for copy in plan:
            copy.wait_recv()
        results = []
        for index, value in enumerate(values):
            solid = value.reshape(N, N, height)
            from_x = x_in[which][:, index]
            first_y = y_in[which][0, index * N : index * N + N, :]
            last_y = y_in[which][1, index * N : index * N + N, :]
            corner = [c_in[which][which_one, index : index + 1, :] for which_one in range(4)]
            first_y = first_y + jnp.where(row_of_x == 0, corner[0], 0.0)
            last_y = last_y + jnp.where(row_of_x == 0, corner[1], 0.0)
            first_y = first_y + jnp.where(row_of_x == N - 1, corner[2], 0.0)
            last_y = last_y + jnp.where(row_of_x == N - 1, corner[3], 0.0)
            slabs = []
            for x in range(N):
                slab = solid[x]
                if x == 0:
                    slab = slab + from_x[0]
                if x == N - 1:
                    slab = slab + from_x[1]
                slab = slab + jnp.where(row_of_x == 0, first_y[x : x + 1, :], 0.0)
                slab = slab + jnp.where(row_of_x == N - 1, last_y[x : x + 1, :], 0.0)
                slabs.append(slab)
            results.append(jnp.concatenate(slabs, axis=0))
        return results

    def spread(which, row):
        row_out[which] = row
        gathered[which, pl.ds(me, 1), :] = row

        def send(step, carry):
            other = lax.rem(me + step, devices)
            pltpu.make_async_remote_copy(
                src_ref=row_out.at[which],
                dst_ref=gathered.at[which, pl.ds(me, 1), :],
                send_sem=row_send.at[which],
                recv_sem=row_recv.at[which],
                device_id=(other // parts_y, lax.rem(other, parts_y)),
                device_id_type=MESH,
            ).start()
            return carry

        lax.fori_loop(1, devices, send, 0)

    def all_rows(which):
        return pltpu.make_async_remote_copy(
            src_ref=gathered.at[which, pl.ds(0, devices - 1), :],
            dst_ref=gathered.at[which, pl.ds(0, devices - 1), :],
            send_sem=row_send.at[which],
            recv_sem=row_recv.at[which],
            device_id=(after_x, my_y),
            device_id_type=MESH,
        )

    def collect(which):
        all_rows(which).wait_recv()
        return gathered[which]

    mass, weight_xy, weight_z = block(MASS), block(WXY), block(WZ)
    one_row = lax.broadcasted_iota(jnp.int32, (1, height), 1)

    def operate(values):
        xy = left_exact(values, DX, KXY + 1)
        z = right_exact(values, ZD, ZK + 1)
        image = xy[2 * points :] * weight_z + weight_xy * z[:, height:]
        gradient = [mass * xy[:points], mass * xy[points : 2 * points], mass * z[:, :height]]
        return image + helmholtz_shift * mass * values, gradient

    def coarse_send(which, residual):
        high, low, rest = split_thrice(residual)
        stacked = jnp.concatenate([high, low, high, low, rest], axis=1)
        table = right_exact_ref[:, ZRESTRICT * height : (ZRESTRICT + 1) * height]
        terms = block(CORNERS) * product(stacked, table)
        spread(which, jnp.sum(terms, axis=0, keepdims=True))

    def local_solve(residual):
        modal = right(left(residual, FORWARD, FORWARD + 1), ZFORWARD, ZFORWARD + 1)
        modal = modal * block(SPECTRUM)
        return left(right(modal, ZBACK, ZBACK + 1), BACK, BACK + 1)

    def own_modes(piece):
        sides = block(SIDES)
        next_x, next_y = lax.rem(my_x + 1, parts_x), lax.rem(my_y + 1, parts_y)

        def row(which):
            return rows_ref[piece, pl.ds(which, 1), :]

        own_x = sides[:, 0:1] * row(my_x) + sides[:, 1:2] * row(next_x)
        own_y = sides[:, 2:3] * row(parts_x + my_y) + sides[:, 3:4] * row(parts_x + next_y)
        return split(own_x * own_y)

    pieces = modes_ref.shape[0]
    length = modes_ref.shape[1]
    span = length if pieces == 1 else 2 * length
    mode_lane = lax.broadcasted_iota(jnp.int32, (length, height), 1)
    group = height // 4

    def coarse_piece(piece, stacked, own):
        each = product(vertex_ref[piece, :, :span], stacked[:span])
        for begin in range(span, devices, span):
            lines = slice(begin, begin + span)
            each = each + product(vertex_ref[piece, :, lines], stacked[lines])
        tops, lows = each[: 4 * length], each[4 * length :]
        each = (tops[:, 2 * height :] + lows[:, height : 2 * height]) + (
            tops[:, height : 2 * height] + lows[:, :height]
        )
        each = each + tops[:, :height]
        total = jnp.zeros((length, height), F32)
        for corner in range(4):
            chosen = (mode_lane >= corner * group) & (mode_lane < corner * group + group)
            total = jnp.where(chosen, each[corner * length : (corner + 1) * length], total)
        levels = right(total * modes_ref[piece], ZPROLONG, ZPROLONG + 1)
        high, low = split(levels)
        own_high, own_low = own
        return product(own_high, high) + (product(own_high, low) + product(own_low, high))

    def coarse_finish(which):
        stacked = jnp.concatenate(split_thrice(collect(which)), axis=1)
        if pieces == 1:
            return coarse_piece(0, stacked, own)
        total = jnp.zeros((points, height), F32)
        for piece in range(pieces):
            total = total + coarse_piece(piece, stacked, own_modes(piece))
        return total

    def scalars_send(which, residual, smoothed, image):
        gamma = jnp.sum(residual * smoothed * block(COPIES), axis=0, keepdims=True)
        delta = jnp.sum(smoothed * image, axis=0, keepdims=True)
        gamma = gamma + pltpu.roll(gamma, height // 2, 1)
        delta = delta + pltpu.roll(delta, height // 2, 1)
        spread(which, jnp.where(one_row < height // 2, gamma, delta))

    def scalars_finish(which):
        total = jnp.sum(collect(which), axis=0, keepdims=True)
        gamma = jnp.sum(jnp.where(one_row < height // 2, total, 0.0), axis=1, keepdims=True)
        delta = jnp.sum(jnp.where(one_row < height // 2, 0.0, total), axis=1, keepdims=True)
        return gamma, delta

    flow = [flow_ref[part * points : (part + 1) * points, :] for part in range(4)]
    u, v, w, theta = flow
    xy = left_exact(jnp.concatenate(flow, axis=1), DX, KXY + 1)
    z = right_exact(flow_ref[...], ZD, ZK + 1)
    canopy = jnp.where(lane // N < roof_ref[0, 0], 1.0, 0.0)
    drag = drag_strength * canopy * jnp.sqrt(u * u + v * v + w * w)
    forcing = [-drag * u, -drag * v, -drag * w + buoyancy * theta, heating * canopy]
    rates = []
    for part in range(4):
        lanes = slice(part * height, (part + 1) * height)
        rows = slice(part * points, (part + 1) * points)
        advection = u * xy[:points, lanes] + v * xy[points : 2 * points, lanes] + w * z[rows, :height]
        friction = xy[2 * points :, lanes] * weight_z + weight_xy * z[rows, height:]
        rates.append(mass * (forcing[part] - advection) - viscosity * friction)
    pl.semaphore_wait(barrier, devices - 1)
    rates = start(0, rates)

    old = old_ref[...]
    old_image, old_gradient = operate(old)
    own = own_modes(0) if pieces == 1 else None

    rates = finish(0, rates)
    step = block(STEP)
    provisional = [values + step * rate for values, rate in zip(flow, rates)]
    provisional[2] = jnp.where((lane == 0) | (lane == height - 1), 0.0, provisional[2])
    divergence = (
        left_exact(provisional[0], DX, DX + 1)
        + left_exact(provisional[1], DY, DY + 1)
        + right_exact(provisional[2], ZD, ZD + 1)
    )
    residual = finish(1, start(1, [-mass * divergence - old_image]))[0]

    coarse_send(0, residual)
    local = start(2, [local_solve(residual)])
    coarse = coarse_finish(0)
    first = finish(2, local)[0] + coarse
    image, first_gradient = operate(first)
    scalars_send(1, residual, first, image)
    image = start(3, [image])
    gradients = start(6, old_gradient + first_gradient)
    gamma_first, delta_first = scalars_finish(1)
    alpha_first = gamma_first / delta_first
    residual = residual - alpha_first * finish(3, image)[0]

    coarse_send(2, residual)
    local = start(4, [local_solve(residual)])
    coarse = coarse_finish(2)
    second = finish(4, local)[0] + coarse
    image, second_gradient = operate(second)
    scalars_send(3, residual, second, image)
    second_gradient = start(5, second_gradient)
    gradients = finish(6, gradients)
    gamma, delta = scalars_finish(3)
    ratio = gamma / gamma_first
    alpha = gamma / (delta - ratio * gamma / alpha_first)
    weight_first = alpha_first + alpha * ratio
    pressure_ref[...] = old + weight_first * first + alpha * second
    state_ref[3 * points : 4 * points, :] = provisional[3]
    second_gradient = finish(5, second_gradient)
    inverse = block(INVERSE)
    for part in range(3):
        total = gradients[part] + weight_first * gradients[3 + part] + alpha * second_gradient[part]
        state_ref[part * points : (part + 1) * points, :] = provisional[part] - total * inverse

    for which in range(count):
        for copy in copies(which):
            copy.wait_send()
    for which in range(GATHERS):
        all_rows(which).wait_send()


def on_device(flow_state, building_height, pressure_old):
    parts = (lax.axis_size("gx"), lax.axis_size("gy"))
    devices = parts[0] * parts[1]
    components, width, depth, height = flow_state.shape
    points = width * depth
    assert width == N and depth == N and components == 4
    tables = constants(parts[0], parts[1], height)
    scratch = [pltpu.VMEM((number, points, height), F32) for number in EXCHANGES]
    scratch += [pltpu.VMEM((2, number * N, height), F32) for number in EXCHANGES]
    scratch += [pltpu.VMEM((4, number, height), F32) for number in EXCHANGES]
    scratch += [pltpu.VMEM((2, number, N, height), F32) for number in EXCHANGES]
    scratch += [pltpu.VMEM((2, number * N, height), F32) for number in EXCHANGES]
    scratch += [pltpu.VMEM((4, number, height), F32) for number in EXCHANGES]
    scratch += [
        pltpu.VMEM((GATHERS, 1, height), F32),
        pltpu.VMEM((GATHERS, devices, height), F32),
        pltpu.SemaphoreType.DMA((len(EXCHANGES), 8)),
        pltpu.SemaphoreType.DMA((len(EXCHANGES), 8)),
        pltpu.SemaphoreType.DMA((GATHERS,)),
        pltpu.SemaphoreType.DMA((GATHERS,)),
    ]
    whole = pl.BlockSpec(memory_space=pltpu.VMEM)
    scalar = pl.BlockSpec(memory_space=pltpu.SMEM)
    state, pressure = pl.pallas_call(
        functools.partial(kernel, parts),
        out_shape=(
            jax.ShapeDtypeStruct((components * points, height), F32),
            jax.ShapeDtypeStruct((points, height), F32),
        ),
        in_specs=[whole, scalar] + [whole] * 9,
        out_specs=(whole, whole),
        scratch_shapes=scratch,
        compiler_params=pltpu.CompilerParams(
            collective_id=0, has_side_effects=True, vmem_limit_bytes=48 * 2**20
        ),
    )(
        flow_state.reshape(components * points, height),
        building_height,
        pressure_old.reshape(points, height),
        *[jnp.asarray(table) for table in tables],
    )
    return state.reshape(flow_state.shape), pressure.reshape(pressure_old.shape)


def solution(mesh):
    in_specs = (P(None, "gx", "gy", None), P("gx", "gy"), P("gx", "gy", None))
    out_specs = (P(None, "gx", "gy", None), P("gx", "gy", None))
    return jax.shard_map(
        on_device, mesh=mesh, in_specs=in_specs, out_specs=out_specs, check_vma=False
    )
```

time: 310 us -> 49 us (0.16)
  blocking collectives: 159 us -> 0 us
  starting transfers between devices: 53.6 us -> 0 us
  Pallas kernels: 0 us -> 38 us
  local copies, waits for them, and re-layouts: 30.6 us -> 9.22 us
  matrix products: 19.6 us -> 0 us
  other arithmetic: 18.8 us -> 0 us
  waiting for transfers between devices: 16.1 us -> 0 us
  between operations: 9.26 us -> 1.31 us
    all_gather x2 -> x0, blocking collectives: 80 us -> none  [coarse_whole(): lax.all_gather(piece.reshape(1, rows * columns * levels), ('gx', 'gy'), a...]
    psum x2 -> x0, blocking collectives: 79.1 us -> none  [paired_sums(): lax.psum((jnp.sum(residual * smoothed / counts), jnp.sum(image * smoothed...]
    ppermute x32 -> x0, starting transfers between devices: 53.6 us -> none  [the longest x16 47.8 us: padded_2(): lax.ppermute(head, axis, [((i + 1) % count, i) for i in range(count)])]
    pallas_call x0 -> x1, Pallas kernels: none -> 38 us  [on_device(): pl.pallas_call(functools.partial(kernel, parts), out_shape=(jax.ShapeDtyp...]
    dot_general x70 -> x0, matrix products: 18.5 us -> none  [the longest x14 4.49 us: along_z(): return jnp.dot(rows, banded.T, precision=HIGHEST).reshape(field.shape)]
    ppermute x32 -> x0, waiting for transfers between devices: 16.1 us -> none  [the longest x16 15.7 us: padded_2(): lax.ppermute(tail, axis, [(i, (i + 1) % count) for i in range(count)])]
    unnamed x138 -> x22, local copies, waits for them, and re-layouts: 16.5 us -> 9.22 us
    slice x72 -> x0, local copies, waits for them, and re-layouts: 5.8 us -> none  [the longest x12 1.85 us: pair_y_padded(): inner[:, :, :, 1:7]]
  transfers between devices with their start and end apart: 32 -> 0, of which waited for: 12 -> 0; matrix products, arithmetic and copies ran while one was open for 8% -> 0% of each run, Pallas kernels for 0% -> 0%
where the time goes in v1:
time: 49 us; the launch traced here: 48.5 us
  Pallas kernels  38 us (78%)
  local copies, waits for them, and re-layouts  9.22 us (19%)
  between operations  1.31 us (3%)
    pallas_call x1, Pallas kernels, on_device(): pl.pallas_call(functools.partial(kernel, parts), out_shape=(jax.ShapeDtyp...  38 us
    unnamed x22, local copies, waits for them, and re-layouts  9.22 us

profile of v1, /device:TPU:0, one launch (start us, length us, event | category | flops | bytes accessed | tf_op | source)
XLA Modules:
  0.0 48.5 jit_solution(15157482239479766111)
XLA Ops:
  0.6 0.0 copy-start.8
  1.3 0.1 copy-done.8
  1.4 0.0 copy-start
  1.4 1.0 %copy-done = bf16[640,384]{1,0:T(8,128)(2,1)S(1)} copy-done((bf16[640,384]{1,0:T(8,128)(2,1)S(1)}, bf16[640,384]{1,0:T(8,128)(2,1)}, u32[]{:S(2)}) %copy-start) | copy-done | bytes 491544
  2.4 0.0 copy-start.1
  2.4 1.0 %copy-done.1 = f32[576,128]{1,0:T(8,128)S(1)} copy-done((f32[576,128]{1,0:T(8,128)S(1)}, f32[576,128]{1,0:T(8,128)}, u32[]{:S(2)}) %copy-start.1) | copy-done | bytes 294936
  3.3 0.0 copy-start.2
  3.3 1.0 %copy-done.2 = bf16[384,384]{1,0:T(8,128)(2,1)S(1)} copy-done((bf16[384,384]{1,0:T(8,128)(2,1)S(1)}, bf16[384,384]{1,0:T(8,128)(2,1)}, u32[]{:S(2)}) %copy-start.2) | copy-done | bytes 294936
  4.3 0.0 copy-start.3
  4.3 0.9 %copy-done.3 = bf16[192,320]{1,0:T(8,128)(2,1)S(1)} copy-done((bf16[192,320]{1,0:T(8,128)(2,1)S(1)}, bf16[192,320]{1,0:T(8,128)(2,1)}, u32[]{:S(2)}) %copy-start.3) | copy-done | bytes 122904
  5.2 0.0 copy-start.4
  5.2 0.9 %copy-done.4 = f32[4,8,8,128]{3,2,1,0:T(8,128)S(1)} copy-done((f32[4,8,8,128]{3,2,1,0:T(8,128)S(1)}, f32[4,8,8,128]{3,2,1,0:T(8,128)}, u32[]{:S(2)}) %copy-start.4) | copy-done | bytes 131096
  6.1 0.0 copy-start.5
  6.1 0.8 %copy-done.5 = bf16[1,256,32]{2,1,0:T(8,128)(2,1)S(1)} copy-done((bf16[1,256,32]{2,1,0:T(8,128)(2,1)S(1)}, bf16[1,256,32]{2,1,0:T(8,128)(2,1)}, u32[]{:S(2)}) %copy-start.5) | copy-done | bytes 16408
  7.0 0.0 copy-start.6
  7.0 0.8 %copy-done.6 = bf16[128,256]{1,0:T(8,128)(2,1)S(1)} copy-done((bf16[128,256]{1,0:T(8,128)(2,1)S(1)}, bf16[128,256]{1,0:T(8,128)(2,1)}, u32[]{:S(2)}) %copy-start.6) | copy-done | bytes 65560
  7.8 0.0 copy-start.7
  7.8 0.8 %copy-done.7 = f32[8,8,128]{2,1,0:T(8,128)S(1)} copy-done((f32[8,8,128]{2,1,0:T(8,128)S(1)}, f32[8,8,128]{2,1,0:T(8,128)}, u32[]{:S(2)}) %copy-start.7) | copy-done | bytes 32792
  8.6 0.0 copy-start.9
  8.6 0.7 %copy-done.9 = f32[1,12,32]{2,1,0:T(8,128)S(1)} copy-done((f32[1,12,32]{2,1,0:T(8,128)S(1)}, f32[1,12,32]{2,1,0:T(8,128)}, u32[]{:S(2)}) %copy-start.9) | copy-done | bytes 1560
  9.3 38.0 %shard_map.122 = (f32[256,128]{1,0:T(8,128)S(1)}, f32[64,128]{1,0:T(8,128)S(1)}) custom-call(f32[256,128]{1,0:T(8,128)S(1)} %bitcast.5, s32[1,1]{1,0:T(1,128)S(6)} %copy.15.roof_ref, f32[64,128]{1,0:T(8,128)S(1)} %bitcast.6, bf16[192,320]{1,0:T(8,128)(2,1)S(1)} %copy-done.3, bf16[640,384]{1,0:T(8,128)(2,1)S(1)} %copy-done, bf16[128,256]{1,0:T(8,128)(2,1)S(1)} %copy-done.6, ...), custom_call_target="tpu_custom_call" | custom-call | tf_op jit(solution)/shard_map/pallas_call | solution.py:590
  47.2 0.7 %copy.16 = f32[4,8,8,128]{3,2,1,0:T(8,128)} copy(f32[4,8,8,128]{3,2,1,0:T(8,128)S(1)} %bitcast.4) | data formatting | bytes 262144
  47.9 0.6 %copy.17 = f32[8,8,128]{2,1,0:T(8,128)} copy(f32[8,8,128]{2,1,0:T(8,128)S(1)} %bitcast.7) | data formatting | bytes 65536
Async XLA Ops:
  0.6 0.7 %copy-start.8 = (f32[1,32,128]{2,1,0:T(8,128)S(1)}, f32[1,32,128]{2,1,0:T(8,128)}, u32[]{:S(2)}) copy-start(f32[1,32,128]{2,1,0:T(8,128)} %constant.23.clone.modes_ref) | copy-start | bytes 49156
  1.4 1.0 %copy-start = (bf16[640,384]{1,0:T(8,128)(2,1)S(1)}, bf16[640,384]{1,0:T(8,128)(2,1)}, u32[]{:S(2)}) copy-start(bf16[640,384]{1,0:T(8,128)(2,1)} %constant.17.clone.right_exact_ref) | copy-start | bytes 1474564
  2.4 1.0 %copy-start.1 = (f32[576,128]{1,0:T(8,128)S(1)}, f32[576,128]{1,0:T(8,128)}, u32[]{:S(2)}) copy-start(f32[576,128]{1,0:T(8,128)} %constant.20.clone.plain_ref) | copy-start | bytes 884740
  3.3 1.0 %copy-start.2 = (bf16[384,384]{1,0:T(8,128)(2,1)S(1)}, bf16[384,384]{1,0:T(8,128)(2,1)}, u32[]{:S(2)}) copy-start(bf16[384,384]{1,0:T(8,128)(2,1)} %constant.19.clone.right_ref) | copy-start | bytes 884740
  4.3 0.9 %copy-start.3 = (bf16[192,320]{1,0:T(8,128)(2,1)S(1)}, bf16[192,320]{1,0:T(8,128)(2,1)}, u32[]{:S(2)}) copy-start(bf16[192,320]{1,0:T(8,128)(2,1)} %constant.16.clone.left_exact_ref) | copy-start | bytes 368644
  5.2 0.9 %copy-start.4 = (f32[4,8,8,128]{3,2,1,0:T(8,128)S(1)}, f32[4,8,8,128]{3,2,1,0:T(8,128)}, u32[]{:S(2)}) copy-start(f32[4,8,8,128]{3,2,1,0:T(8,128)} %param.11) | copy-start | bytes 393220
  6.1 0.8 %copy-start.5 = (bf16[1,256,32]{2,1,0:T(8,128)(2,1)S(1)}, bf16[1,256,32]{2,1,0:T(8,128)(2,1)}, u32[]{:S(2)}) copy-start(bf16[1,256,32]{2,1,0:T(8,128)(2,1)} %constant.21.clone.vertex_ref) | copy-start | bytes 49156
  7.0 0.8 %copy-start.6 = (bf16[128,256]{1,0:T(8,128)(2,1)S(1)}, bf16[128,256]{1,0:T(8,128)(2,1)}, u32[]{:S(2)}) copy-start(bf16[128,256]{1,0:T(8,128)(2,1)} %constant.18.clone.left_ref) | copy-start | bytes 196612
  7.8 0.8 %copy-start.7 = (f32[8,8,128]{2,1,0:T(8,128)S(1)}, f32[8,8,128]{2,1,0:T(8,128)}, u32[]{:S(2)}) copy-start(f32[8,8,128]{2,1,0:T(8,128)} %param.13) | copy-start | bytes 98308
  8.6 0.7 %copy-start.9 = (f32[1,12,32]{2,1,0:T(8,128)S(1)}, f32[1,12,32]{2,1,0:T(8,128)}, u32[]{:S(2)}) copy-start(f32[1,12,32]{2,1,0:T(8,128)} %constant.22.clone.rows_ref) | copy-start | bytes 4612

commit v2 on v1

--- a/solution.py
+++ b/solution.py
@@ -117,7 +117,7 @@
     layers = height // N
     levels = layers + 1
     group = height // 4
-    assert levels <= group
+    assert levels + 2 <= group
     eye = np.eye(N)
     diagonal = np.diag(weights)
     stiffness = derivative.T @ diagonal @ derivative
@@ -152,7 +152,7 @@
     rights = [np.kron(many, derivative.T), np.kron(many, stiffness)]
     high, low, rest = thirds(np.concatenate(rights, axis=1))
     right_exact = np.concatenate([high, high, low, low, rest], axis=0)
-    high, low, rest = thirds(grouped / count_z[:, None])
+    high, low, rest = thirds(grouped)
     right_exact = np.concatenate(
         [right_exact, np.concatenate([high, high, low, low, high], axis=0)], axis=1
     )
@@ -171,7 +171,7 @@
     sides = np.zeros((N * N, height))
     sides[:, 0], sides[:, 1], sides[:, 2], sides[:, 3] = near_x, far_x, near_y, far_y
     corner = np.stack([near_x * near_y, near_x * far_y, far_x * near_y, far_x * far_y], axis=1)
-    corners = np.repeat(corner / count_xy[:, None], group, axis=1)
+    corners = np.repeat(corner, group, axis=1)
     plain = np.concatenate(
         [
             mass,
@@ -230,26 +230,37 @@
 
 
 EXCHANGES = (4, 1, 1, 1, 1, 3, 6)
-GATHERS = 4
+GATHERS = 3
+OPERANDS = 11
 
 
 def kernel(
     parts,
-    flow_ref,
-    roof_ref,
-    old_ref,
-    left_exact_ref,
-    right_exact_ref,
-    left_ref,
-    right_ref,
-    plain_ref,
-    vertex_ref,
-    rows_ref,
-    modes_ref,
-    state_ref,
-    pressure_ref,
-    *scratch,
+    *refs,
 ):
+    operands, (state_ref, pressure_ref) = refs[:OPERANDS], refs[OPERANDS : OPERANDS + 2]
+    held = refs[OPERANDS + 2 : 2 * OPERANDS + 2]
+    load_sem, *scratch = refs[2 * OPERANDS + 2 :]
+    loads = [
+        pltpu.make_async_copy(source, here, load_sem.at[index])
+        for index, (source, here) in enumerate(zip(operands, held))
+    ]
+    for load in loads:
+        load.start()
+    (
+        flow_ref,
+        left_exact_ref,
+        right_exact_ref,
+        plain_ref,
+        roof_ref,
+        old_ref,
+        rows_ref,
+        left_ref,
+        right_ref,
+        vertex_ref,
+        modes_ref,
+    ) = held
+
     parts_x, parts_y = parts
     devices = parts_x * parts_y
     count = len(EXCHANGES)
@@ -268,14 +279,25 @@
 
     barrier = pltpu.get_barrier_semaphore()
 
-    def greet(step, carry):
-        other = lax.rem(me + step, devices)
-        pl.semaphore_signal(
-            barrier, inc=1, device_id=(other // parts_y, lax.rem(other, parts_y)), device_id_type=MESH
-        )
-        return carry
-
-    lax.fori_loop(1, devices, greet, 0)
+    def each_other(action):
+        if devices <= 64:
+            all_x = [lax.rem(my_x + step, parts_x) for step in range(parts_x)]
+            all_y = [lax.rem(my_y + step, parts_y) for step in range(parts_y)]
+            for step in range(1, devices):
+                action(all_x[step // parts_y], all_y[step % parts_y])
+            return
+
+        def one(step, carry):
+            other = lax.rem(me + step, devices)
+            action(other // parts_y, lax.rem(other, parts_y))
+            return carry
+
+        lax.fori_loop(1, devices, one, 0)
+
+    def greet(other_x, other_y):
+        pl.semaphore_signal(barrier, inc=1, device_id=(other_x, other_y), device_id_type=MESH)
+
+    each_other(greet)
 
     before_x, after_x = lax.rem(my_x + parts_x - 1, parts_x), lax.rem(my_x + 1, parts_x)
     before_y, after_y = lax.rem(my_y + parts_y - 1, parts_y), lax.rem(my_y + 1, parts_y)
@@ -385,19 +407,17 @@
         row_out[which] = row
         gathered[which, pl.ds(me, 1), :] = row
 
-        def send(step, carry):
-            other = lax.rem(me + step, devices)
+        def send(other_x, other_y):
             pltpu.make_async_remote_copy(
                 src_ref=row_out.at[which],
                 dst_ref=gathered.at[which, pl.ds(me, 1), :],
                 send_sem=row_send.at[which],
                 recv_sem=row_recv.at[which],
-                device_id=(other // parts_y, lax.rem(other, parts_y)),
+                device_id=(other_x, other_y),
                 device_id_type=MESH,
             ).start()
-            return carry
-
-        lax.fori_loop(1, devices, send, 0)
+
+        each_other(send)
 
     def all_rows(which):
         return pltpu.make_async_remote_copy(
@@ -413,8 +433,9 @@
         all_rows(which).wait_recv()
         return gathered[which]
 
-    mass, weight_xy, weight_z = block(MASS), block(WXY), block(WZ)
     one_row = lax.broadcasted_iota(jnp.int32, (1, height), 1)
+    group = height // 4
+    spare = height // N + 1
 
     def operate(values):
         xy = left_exact(values, DX, KXY + 1)
@@ -423,12 +444,23 @@
         gradient = [mass * xy[:points], mass * xy[points : 2 * points], mass * z[:, :height]]
         return image + helmholtz_shift * mass * values, gradient
 
-    def coarse_send(which, residual):
-        high, low, rest = split_thrice(residual)
+    def coarse_row(part):
+        high, low, rest = split_thrice(part)
         stacked = jnp.concatenate([high, low, high, low, rest], axis=1)
         table = right_exact_ref[:, ZRESTRICT * height : (ZRESTRICT + 1) * height]
         terms = block(CORNERS) * product(stacked, table)
-        spread(which, jnp.sum(terms, axis=0, keepdims=True))
+        return jnp.sum(terms, axis=0, keepdims=True)
+
+    def with_scalars(row, residual, smoothed, image):
+        gamma = jnp.sum(residual * smoothed * block(COPIES), axis=0, keepdims=True)
+        delta = jnp.sum(smoothed * image, axis=0, keepdims=True)
+        gamma = jnp.sum(gamma, axis=1, keepdims=True)
+        delta = jnp.sum(delta, axis=1, keepdims=True)
+        return jnp.where(one_row == spare, gamma, jnp.where(one_row == spare + 1, delta, row))
+
+    def scalars(rows):
+        total = jnp.sum(rows, axis=0, keepdims=True)
+        return total[:, spare : spare + 1], total[:, spare + 1 : spare + 2]
 
     def local_solve(residual):
         modal = right(left(residual, FORWARD, FORWARD + 1), ZFORWARD, ZFORWARD + 1)
@@ -450,7 +482,6 @@
     length = modes_ref.shape[1]
     span = length if pieces == 1 else 2 * length
     mode_lane = lax.broadcasted_iota(jnp.int32, (length, height), 1)
-    group = height // 4
 
     def coarse_piece(piece, stacked, own):
         each = product(vertex_ref[piece, :, :span], stacked[:span])
@@ -471,8 +502,8 @@
         own_high, own_low = own
         return product(own_high, high) + (product(own_high, low) + product(own_low, high))
 
-    def coarse_finish(which):
-        stacked = jnp.concatenate(split_thrice(collect(which)), axis=1)
+    def coarse_solve(rows):
+        stacked = jnp.concatenate(split_thrice(rows), axis=1)
         if pieces == 1:
             return coarse_piece(0, stacked, own)
         total = jnp.zeros((points, height), F32)
@@ -480,24 +511,14 @@
             total = total + coarse_piece(piece, stacked, own_modes(piece))
         return total
 
-    def scalars_send(which, residual, smoothed, image):
-        gamma = jnp.sum(residual * smoothed * block(COPIES), axis=0, keepdims=True)
-        delta = jnp.sum(smoothed * image, axis=0, keepdims=True)
-        gamma = gamma + pltpu.roll(gamma, height // 2, 1)
-        delta = delta + pltpu.roll(delta, height // 2, 1)
-        spread(which, jnp.where(one_row < height // 2, gamma, delta))
-
-    def scalars_finish(which):
-        total = jnp.sum(collect(which), axis=0, keepdims=True)
-        gamma = jnp.sum(jnp.where(one_row < height // 2, total, 0.0), axis=1, keepdims=True)
-        delta = jnp.sum(jnp.where(one_row < height // 2, 0.0, total), axis=1, keepdims=True)
-        return gamma, delta
-
+    for load in loads[:5]:
+        load.wait()
+    mass, weight_xy, weight_z = block(MASS), block(WXY), block(WZ)
     flow = [flow_ref[part * points : (part + 1) * points, :] for part in range(4)]
     u, v, w, theta = flow
     xy = left_exact(jnp.concatenate(flow, axis=1), DX, KXY + 1)
     z = right_exact(flow_ref[...], ZD, ZK + 1)
-    canopy = jnp.where(lane // N < roof_ref[0, 0], 1.0, 0.0)
+    canopy = jnp.where(lane // N < roof_ref[...], 1.0, 0.0)
     drag = drag_strength * canopy * jnp.sqrt(u * u + v * v + w * w)
     forcing = [-drag * u, -drag * v, -drag * w + buoyancy * theta, heating * canopy]
     rates = []
@@ -510,6 +531,8 @@
     pl.semaphore_wait(barrier, devices - 1)
     rates = start(0, rates)
 
+    for load in loads[5:]:
+        load.wait()
     old = old_ref[...]
     old_image, old_gradient = operate(old)
     own = own_modes(0) if pieces == 1 else None
@@ -523,29 +546,32 @@
         + left_exact(provisional[1], DY, DY + 1)
         + right_exact(provisional[2], ZD, ZD + 1)
     )
-    residual = finish(1, start(1, [-mass * divergence - old_image]))[0]
-
-    coarse_send(0, residual)
+    raw = -mass * divergence - old_image
+    whole = start(1, [raw])
+    spread(0, coarse_row(raw))
+    residual = finish(1, whole)[0]
+
     local = start(2, [local_solve(residual)])
-    coarse = coarse_finish(0)
+    coarse = coarse_solve(collect(0))
     first = finish(2, local)[0] + coarse
-    image, first_gradient = operate(first)
-    scalars_send(1, residual, first, image)
-    image = start(3, [image])
+    raw, first_gradient = operate(first)
+    image = start(3, [raw])
+    spread(1, with_scalars(coarse_row(raw), residual, first, raw))
     gradients = start(6, old_gradient + first_gradient)
-    gamma_first, delta_first = scalars_finish(1)
+    image = finish(3, image)[0]
+
+    local = start(4, [local_solve(image)])
+    rows = collect(1)
+    coarse = coarse_solve(rows)
+    gamma_first, delta_first = scalars(rows)
     alpha_first = gamma_first / delta_first
-    residual = residual - alpha_first * finish(3, image)[0]
-
-    coarse_send(2, residual)
-    local = start(4, [local_solve(residual)])
-    coarse = coarse_finish(2)
-    second = finish(4, local)[0] + coarse
-    image, second_gradient = operate(second)
-    scalars_send(3, residual, second, image)
+    residual = residual - alpha_first * image
+    second = first - alpha_first * (finish(4, local)[0] + coarse)
+    raw, second_gradient = operate(second)
+    spread(2, with_scalars(jnp.zeros((1, height), F32), residual, second, raw))
     second_gradient = start(5, second_gradient)
     gradients = finish(6, gradients)
-    gamma, delta = scalars_finish(3)
+    gamma, delta = scalars(collect(2))
     ratio = gamma / gamma_first
     alpha = gamma / (delta - ratio * gamma / alpha_first)
     weight_first = alpha_first + alpha * ratio
@@ -571,7 +597,25 @@
     points = width * depth
     assert width == N and depth == N and components == 4
     tables = constants(parts[0], parts[1], height)
-    scratch = [pltpu.VMEM((number, points, height), F32) for number in EXCHANGES]
+    left_exact, right_exact, left, right, plain, vertex, rows, modes = [
+        jnp.asarray(table) for table in tables
+    ]
+    operands = [
+        flow_state.reshape(components * points, height),
+        left_exact,
+        right_exact,
+        plain,
+        building_height,
+        pressure_old.reshape(points, height),
+        rows,
+        left,
+        right,
+        vertex,
+        modes,
+    ]
+    scratch = [pltpu.VMEM(operand.shape, operand.dtype) for operand in operands]
+    scratch += [pltpu.SemaphoreType.DMA((len(operands),))]
+    scratch += [pltpu.VMEM((number, points, height), F32) for number in EXCHANGES]
     scratch += [pltpu.VMEM((2, number * N, height), F32) for number in EXCHANGES]
     scratch += [pltpu.VMEM((4, number, height), F32) for number in EXCHANGES]
     scratch += [pltpu.VMEM((2, number, N, height), F32) for number in EXCHANGES]
@@ -586,25 +630,19 @@
         pltpu.SemaphoreType.DMA((GATHERS,)),
     ]
     whole = pl.BlockSpec(memory_space=pltpu.VMEM)
-    scalar = pl.BlockSpec(memory_space=pltpu.SMEM)
     state, pressure = pl.pallas_call(
         functools.partial(kernel, parts),
         out_shape=(
             jax.ShapeDtypeStruct((components * points, height), F32),
             jax.ShapeDtypeStruct((points, height), F32),
         ),
-        in_specs=[whole, scalar] + [whole] * 9,
+        in_specs=[pl.BlockSpec(memory_space=pltpu.HBM)] * len(operands),
         out_specs=(whole, whole),
         scratch_shapes=scratch,
         compiler_params=pltpu.CompilerParams(
             collective_id=0, has_side_effects=True, vmem_limit_bytes=48 * 2**20
         ),
-    )(
-        flow_state.reshape(components * points, height),
-        building_height,
-        pressure_old.reshape(points, height),
-        *[jnp.asarray(table) for table in tables],
-    )
+    )(*operands)
     return state.reshape(flow_state.shape), pressure.reshape(pressure_old.shape)
 
 

time: 49 us -> 47.4 us (0.967)
  Pallas kernels: 38 us -> 36.3 us
    pallas_call x1, Pallas kernels: 38 us -> 36.3 us  [on_device(): pl.pallas_call(functools.partial(kernel, parts), out_shape=(jax.ShapeDtyp...]
where the time goes in v2:
time: 47.4 us; the launch traced here: 46.9 us
  Pallas kernels  36.3 us (77%)
  local copies, waits for them, and re-layouts  9.22 us (19%)
  between operations  1.31 us (3%)
    pallas_call x1, Pallas kernels, on_device(): pl.pallas_call(functools.partial(kernel, parts), out_shape=(jax.ShapeDtyp...  36.3 us
    unnamed x22, local copies, waits for them, and re-layouts  9.22 us

profile of v2, /device:TPU:0, one launch (start us, length us, event | category | flops | bytes accessed | tf_op | source)
XLA Modules:
  0.0 46.9 jit_solution(4975771777354588808)
XLA Ops:
  0.6 0.0 copy-start.8
  1.3 0.1 copy-done.8
  1.4 0.0 copy-start
  1.4 1.0 %copy-done = bf16[640,384]{1,0:T(8,128)(2,1)S(1)} copy-done((bf16[640,384]{1,0:T(8,128)(2,1)S(1)}, bf16[640,384]{1,0:T(8,128)(2,1)}, u32[]{:S(2)}) %copy-start) | copy-done | bytes 491544
  2.4 0.0 copy-start.1
  2.4 1.0 %copy-done.1 = f32[576,128]{1,0:T(8,128)S(1)} copy-done((f32[576,128]{1,0:T(8,128)S(1)}, f32[576,128]{1,0:T(8,128)}, u32[]{:S(2)}) %copy-start.1) | copy-done | bytes 294936
  3.3 0.0 copy-start.2
  3.3 1.0 %copy-done.2 = bf16[384,384]{1,0:T(8,128)(2,1)S(1)} copy-done((bf16[384,384]{1,0:T(8,128)(2,1)S(1)}, bf16[384,384]{1,0:T(8,128)(2,1)}, u32[]{:S(2)}) %copy-start.2) | copy-done | bytes 294936
  4.3 0.0 copy-start.3
  4.3 0.9 %copy-done.3 = bf16[192,320]{1,0:T(8,128)(2,1)S(1)} copy-done((bf16[192,320]{1,0:T(8,128)(2,1)S(1)}, bf16[192,320]{1,0:T(8,128)(2,1)}, u32[]{:S(2)}) %copy-start.3) | copy-done | bytes 122904
  5.2 0.0 copy-start.4
  5.2 0.9 %copy-done.4 = f32[4,8,8,128]{3,2,1,0:T(8,128)S(1)} copy-done((f32[4,8,8,128]{3,2,1,0:T(8,128)S(1)}, f32[4,8,8,128]{3,2,1,0:T(8,128)}, u32[]{:S(2)}) %copy-start.4) | copy-done | bytes 131096
  6.1 0.0 copy-start.5
  6.1 0.8 %copy-done.5 = bf16[1,256,32]{2,1,0:T(8,128)(2,1)S(1)} copy-done((bf16[1,256,32]{2,1,0:T(8,128)(2,1)S(1)}, bf16[1,256,32]{2,1,0:T(8,128)(2,1)}, u32[]{:S(2)}) %copy-start.5) | copy-done | bytes 16408
  7.0 0.0 copy-start.6
  7.0 0.8 %copy-done.6 = bf16[128,256]{1,0:T(8,128)(2,1)S(1)} copy-done((bf16[128,256]{1,0:T(8,128)(2,1)S(1)}, bf16[128,256]{1,0:T(8,128)(2,1)}, u32[]{:S(2)}) %copy-start.6) | copy-done | bytes 65560
  7.8 0.0 copy-start.7
  7.8 0.8 %copy-done.7 = f32[8,8,128]{2,1,0:T(8,128)S(1)} copy-done((f32[8,8,128]{2,1,0:T(8,128)S(1)}, f32[8,8,128]{2,1,0:T(8,128)}, u32[]{:S(2)}) %copy-start.7) | copy-done | bytes 32792
  8.6 0.0 copy-start.9
  8.6 0.7 %copy-done.9 = f32[1,12,32]{2,1,0:T(8,128)S(1)} copy-done((f32[1,12,32]{2,1,0:T(8,128)S(1)}, f32[1,12,32]{2,1,0:T(8,128)}, u32[]{:S(2)}) %copy-start.9) | copy-done | bytes 1560
  9.3 36.3 %shard_map.122 = (f32[256,128]{1,0:T(8,128)S(1)}, f32[64,128]{1,0:T(8,128)S(1)}) custom-call(f32[256,128]{1,0:T(8,128)S(1)} %bitcast.5, bf16[192,320]{1,0:T(8,128)(2,1)S(1)} %copy-done.3, bf16[640,384]{1,0:T(8,128)(2,1)S(1)} %copy-done, f32[576,128]{1,0:T(8,128)S(1)} %copy-done.1, s32[1,1]{1,0:T(1,128)S(6)} %copy.15.refs_4_, f32[64,128]{1,0:T(8,128)S(1)} %bitcast.6, ...), custom_call_target="tpu_custom_call" | custom-call | tf_op jit(solution)/shard_map/pallas_call | solution.py:633
  45.6 0.7 %copy.16 = f32[4,8,8,128]{3,2,1,0:T(8,128)} copy(f32[4,8,8,128]{3,2,1,0:T(8,128)S(1)} %bitcast.4) | data formatting | bytes 262144
  46.2 0.6 %copy.17 = f32[8,8,128]{2,1,0:T(8,128)} copy(f32[8,8,128]{2,1,0:T(8,128)S(1)} %bitcast.7) | data formatting | bytes 65536
Async XLA Ops:
  0.6 0.7 %copy-start.8 = (f32[1,32,128]{2,1,0:T(8,128)S(1)}, f32[1,32,128]{2,1,0:T(8,128)}, u32[]{:S(2)}) copy-start(f32[1,32,128]{2,1,0:T(8,128)} %constant.23.clone.refs_10_) | copy-start | bytes 49156
  1.4 1.0 %copy-start = (bf16[640,384]{1,0:T(8,128)(2,1)S(1)}, bf16[640,384]{1,0:T(8,128)(2,1)}, u32[]{:S(2)}) copy-start(bf16[640,384]{1,0:T(8,128)(2,1)} %constant.17.clone.refs_2_) | copy-start | bytes 1474564
  2.4 1.0 %copy-start.1 = (f32[576,128]{1,0:T(8,128)S(1)}, f32[576,128]{1,0:T(8,128)}, u32[]{:S(2)}) copy-start(f32[576,128]{1,0:T(8,128)} %constant.20.clone.refs_3_) | copy-start | bytes 884740
  3.3 1.0 %copy-start.2 = (bf16[384,384]{1,0:T(8,128)(2,1)S(1)}, bf16[384,384]{1,0:T(8,128)(2,1)}, u32[]{:S(2)}) copy-start(bf16[384,384]{1,0:T(8,128)(2,1)} %constant.19.clone.refs_8_) | copy-start | bytes 884740
  4.3 0.9 %copy-start.3 = (bf16[192,320]{1,0:T(8,128)(2,1)S(1)}, bf16[192,320]{1,0:T(8,128)(2,1)}, u32[]{:S(2)}) copy-start(bf16[192,320]{1,0:T(8,128)(2,1)} %constant.16.clone.refs_1_) | copy-start | bytes 368644
  5.2 0.9 %copy-start.4 = (f32[4,8,8,128]{3,2,1,0:T(8,128)S(1)}, f32[4,8,8,128]{3,2,1,0:T(8,128)}, u32[]{:S(2)}) copy-start(f32[4,8,8,128]{3,2,1,0:T(8,128)} %param.11) | copy-start | bytes 393220
  6.1 0.8 %copy-start.5 = (bf16[1,256,32]{2,1,0:T(8,128)(2,1)S(1)}, bf16[1,256,32]{2,1,0:T(8,128)(2,1)}, u32[]{:S(2)}) copy-start(bf16[1,256,32]{2,1,0:T(8,128)(2,1)} %constant.21.clone.refs_9_) | copy-start | bytes 49156
  7.0 0.8 %copy-start.6 = (bf16[128,256]{1,0:T(8,128)(2,1)S(1)}, bf16[128,256]{1,0:T(8,128)(2,1)}, u32[]{:S(2)}) copy-start(bf16[128,256]{1,0:T(8,128)(2,1)} %constant.18.clone.refs_7_) | copy-start | bytes 196612
  7.8 0.8 %copy-start.7 = (f32[8,8,128]{2,1,0:T(8,128)S(1)}, f32[8,8,128]{2,1,0:T(8,128)}, u32[]{:S(2)}) copy-start(f32[8,8,128]{2,1,0:T(8,128)} %param.13) | copy-start | bytes 98308
  8.6 0.7 %copy-start.9 = (f32[1,12,32]{2,1,0:T(8,128)S(1)}, f32[1,12,32]{2,1,0:T(8,128)}, u32[]{:S(2)}) copy-start(f32[1,12,32]{2,1,0:T(8,128)} %constant.22.clone.refs_6_) | copy-start | bytes 4612

commit v3 on v2

--- a/solution.py
+++ b/solution.py
@@ -229,7 +229,7 @@
     return jnp.dot(first, second, preferred_element_type=F32)
 
 
-EXCHANGES = (4, 1, 1, 1, 1, 3, 6)
+EXCHANGES = (4, 4, 1, 1, 4, 3)
 GATHERS = 3
 OPERANDS = 11
 
@@ -335,17 +335,17 @@
         return values + jnp.where(joins_up, up, jnp.where(joins_down, down, 0.0))
 
     def copies(which):
-        field, number = fields[which], EXCHANGES[which]
+        field = fields[which]
         plan = []
         x_faces = (field.at[:, points - N : points, :], field.at[:, 0:N, :])
         for side, target in ((0, after_x), (1, before_x)):
             plan.append((x_faces[side], x_in[which].at[side], (target, my_y)))
-        for side, target in ((0, after_y), (1, before_y)):
-            plan.append((y_out[which].at[side], y_in[which].at[side], (my_x, target)))
         for corner, target in enumerate(
             ((after_x, after_y), (after_x, before_y), (before_x, after_y), (before_x, before_y))
         ):
             plan.append((c_out[which].at[corner], c_in[which].at[corner], target))
+        for side, target in ((0, after_y), (1, before_y)):
+            plan.append((y_out[which].at[side], y_in[which].at[side], (my_x, target)))
         return [
             pltpu.make_async_remote_copy(
                 src_ref=source,
@@ -358,29 +358,33 @@
             for index, (source, landing, target) in enumerate(plan)
         ]
 
-    def start(which, values):
-        field, number = fields[which], EXCHANGES[which]
+    def stage(which, values, first=0):
         values = [pair_z(value) for value in values]
-        for index, value in enumerate(values):
-            field[index] = value
+        for index, value in enumerate(values, first):
+            fields[which][index] = value
             solid = value.reshape(N, N, height)
             y_out[which][0, index * N : index * N + N, :] = solid[:, N - 1, :]
             y_out[which][1, index * N : index * N + N, :] = solid[:, 0, :]
             for corner, row in enumerate((points - 1, points - N, N - 1, 0)):
                 c_out[which][corner, index : index + 1, :] = value[row : row + 1, :]
-        plan = copies(which)
-        for copy in plan:
+        return values
+
+    def start(which, values):
+        values = stage(which, values)
+        for copy in copies(which):
             copy.start()
         return values
 
     row_of_x = lax.broadcasted_iota(jnp.int32, (N, height), 0)
 
     def finish(which, values):
-        plan = copies(which)
-        for copy in plan:
+        for copy in copies(which):
             copy.wait_recv()
+        return join(which, values)
+
+    def join(which, values, first=0):
         results = []
-        for index, value in enumerate(values):
+        for index, value in enumerate(values, first):
             solid = value.reshape(N, N, height)
             from_x = x_in[which][:, index]
             first_y = y_in[which][0, index * N : index * N + N, :]
@@ -535,6 +539,7 @@
         load.wait()
     old = old_ref[...]
     old_image, old_gradient = operate(old)
+    old_gradient = stage(1, old_gradient, 1)
     own = own_modes(0) if pieces == 1 else None
 
     rates = finish(0, rates)
@@ -557,7 +562,7 @@
     raw, first_gradient = operate(first)
     image = start(3, [raw])
     spread(1, with_scalars(coarse_row(raw), residual, first, raw))
-    gradients = start(6, old_gradient + first_gradient)
+    first_gradient = stage(4, first_gradient, 1)
     image = finish(3, image)[0]
 
     local = start(4, [local_solve(image)])
@@ -570,7 +575,7 @@
     raw, second_gradient = operate(second)
     spread(2, with_scalars(jnp.zeros((1, height), F32), residual, second, raw))
     second_gradient = start(5, second_gradient)
-    gradients = finish(6, gradients)
+    gradients = join(1, old_gradient, 1) + join(4, first_gradient, 1)
     gamma, delta = scalars(collect(2))
     ratio = gamma / gamma_first
     alpha = gamma / (delta - ratio * gamma / alpha_first)
@@ -640,7 +645,7 @@
         out_specs=(whole, whole),
         scratch_shapes=scratch,
         compiler_params=pltpu.CompilerParams(
-            collective_id=0, has_side_effects=True, vmem_limit_bytes=48 * 2**20
+            collective_id=0, has_side_effects=True, vmem_limit_bytes=60 * 2**20
         ),
     )(*operands)
     return state.reshape(flow_state.shape), pressure.reshape(pressure_old.shape)

time: 47.4 us -> 40.1 us (0.85)
  local copies, waits for them, and re-layouts: 9.22 us -> 2.19 us
    unnamed x22 -> x4, local copies, waits for them, and re-layouts: 9.22 us -> 2.19 us
where the time goes in v3:
time: 40.1 us; the launch traced here: 40 us
  Pallas kernels  36.5 us (91%)
  local copies, waits for them, and re-layouts  2.19 us (5%)
  between operations  1.29 us (3%)
    pallas_call x1, Pallas kernels, on_device(): pl.pallas_call(functools.partial(kernel, parts), out_shape=(jax.ShapeDtyp...  36.5 us
    unnamed x4, local copies, waits for them, and re-layouts  2.19 us

profile of v3, /device:TPU:0, one launch (start us, length us, event | category | flops | bytes accessed | tf_op | source)
XLA Modules:
  0.0 40.0 jit_solution(14899435803406246219)
XLA Ops:
  1.3 36.5 %shard_map.122 = (f32[256,128]{1,0:T(8,128)}, f32[64,128]{1,0:T(8,128)}) custom-call(f32[256,128]{1,0:T(8,128)} %bitcast.5, bf16[192,320]{1,0:T(8,128)(2,1)} %constant.16.clone.refs_1_, bf16[640,384]{1,0:T(8,128)(2,1)} %constant.17.clone.refs_2_, f32[576,128]{1,0:T(8,128)} %constant.20.clone.refs_3_, s32[1,1]{1,0:T(1,128)S(6)} %copy.15.refs_4_, ...), custom_call_target="tpu_custom_call" | custom-call | tf_op jit(solution)/shard_map/pallas_call | solution.py:638
  37.8 0.0 copy-start
  37.8 1.6 %copy.16 = f32[4,8,8,128]{3,2,1,0:T(8,128)} copy(f32[4,8,8,128]{3,2,1,0:T(8,128)} %bitcast.4) | data formatting | bytes 262144
  39.4 0.0 copy-done
  39.4 0.6 %copy.17 = f32[8,8,128]{2,1,0:T(8,128)} copy(f32[8,8,128]{2,1,0:T(8,128)S(1)} %bitcast.7) | data formatting | bytes 65536
Async XLA Ops:
  37.8 1.6 %copy-start = (f32[64,128]{1,0:T(8,128)S(1)}, f32[64,128]{1,0:T(8,128)}, u32[]{:S(2)}) copy-start(f32[64,128]{1,0:T(8,128)} %get-tuple-element.5) | copy-start | bytes 98308

commit v4 on v3

--- a/solution.py
+++ b/solution.py
@@ -270,37 +270,38 @@
     x_in = scratch[3 * count : 4 * count]
     y_in = scratch[4 * count : 5 * count]
     c_in = scratch[5 * count : 6 * count]
-    row_out, gathered, send_sem, recv_sem, row_send, row_recv = scratch[6 * count :]
+    row_out, line, gathered, send_sem, recv_sem, *gather_sems = scratch[6 * count :]
+    row_send, row_recv, line_send, line_recv = gather_sems
     height = old_ref.shape[1]
     points = old_ref.shape[0]
 
     my_x, my_y = lax.axis_index("gx"), lax.axis_index("gy")
-    me = my_x * parts_y + my_y
 
     barrier = pltpu.get_barrier_semaphore()
 
-    def each_other(action):
-        if devices <= 64:
-            all_x = [lax.rem(my_x + step, parts_x) for step in range(parts_x)]
-            all_y = [lax.rem(my_y + step, parts_y) for step in range(parts_y)]
-            for step in range(1, devices):
-                action(all_x[step // parts_y], all_y[step % parts_y])
-            return
-
+    def others(size, mine, action):
         def one(step, carry):
-            other = lax.rem(me + step, devices)
-            action(other // parts_y, lax.rem(other, parts_y))
+            action(lax.rem(mine + step, size))
             return carry
 
-        lax.fori_loop(1, devices, one, 0)
+        if size <= 8:
+            for step in range(1, size):
+                one(step, 0)
+        else:
+            lax.fori_loop(1, size, one, 0)
 
     def greet(other_x, other_y):
         pl.semaphore_signal(barrier, inc=1, device_id=(other_x, other_y), device_id_type=MESH)
 
-    each_other(greet)
-
     before_x, after_x = lax.rem(my_x + parts_x - 1, parts_x), lax.rem(my_x + 1, parts_x)
     before_y, after_y = lax.rem(my_y + parts_y - 1, parts_y), lax.rem(my_y + 1, parts_y)
+
+    others(parts_x, my_x, lambda other: greet(other, my_y))
+    others(parts_y, my_y, lambda other: greet(my_x, other))
+    for corner_x in (after_x, before_x):
+        for corner_y in (after_y, before_y):
+            greet(corner_x, corner_y)
+    greetings = parts_x - 1 + parts_y - 1 + 4
 
     def block(which):
         return plain_ref[which * points : (which + 1) * points, :]
@@ -409,32 +410,61 @@
 
     def spread(which, row):
         row_out[which] = row
-        gathered[which, pl.ds(me, 1), :] = row
-
-        def send(other_x, other_y):
+        line[which, pl.ds(my_y, 1), :] = row
+
+        def send(other_y):
             pltpu.make_async_remote_copy(
                 src_ref=row_out.at[which],
-                dst_ref=gathered.at[which, pl.ds(me, 1), :],
+                dst_ref=line.at[which, pl.ds(my_y, 1), :],
                 send_sem=row_send.at[which],
                 recv_sem=row_recv.at[which],
-                device_id=(other_x, other_y),
+                device_id=(my_x, other_y),
                 device_id_type=MESH,
             ).start()
 
-        each_other(send)
-
-    def all_rows(which):
+        others(parts_y, my_y, send)
+
+    def line_rows(which):
+        rows = line.at[which, pl.ds(0, parts_y - 1), :]
         return pltpu.make_async_remote_copy(
-            src_ref=gathered.at[which, pl.ds(0, devices - 1), :],
-            dst_ref=gathered.at[which, pl.ds(0, devices - 1), :],
+            src_ref=rows,
+            dst_ref=rows,
             send_sem=row_send.at[which],
             recv_sem=row_recv.at[which],
+            device_id=(my_x, after_y),
+            device_id_type=MESH,
+        )
+
+    def relay(which):
+        line_rows(which).wait_recv()
+        here = pl.ds(pl.multiple_of(my_x * parts_y, parts_y), parts_y)
+        gathered[which, here, :] = line[which]
+
+        def send(other_x):
+            pltpu.make_async_remote_copy(
+                src_ref=line.at[which],
+                dst_ref=gathered.at[which, here, :],
+                send_sem=line_send.at[which],
+                recv_sem=line_recv.at[which],
+                device_id=(other_x, my_y),
+                device_id_type=MESH,
+            ).start()
+
+        others(parts_x, my_x, send)
+
+    def all_lines(which):
+        rows = gathered.at[which, pl.ds(0, devices - parts_y), :]
+        return pltpu.make_async_remote_copy(
+            src_ref=rows,
+            dst_ref=rows,
+            send_sem=line_send.at[which],
+            recv_sem=line_recv.at[which],
             device_id=(after_x, my_y),
             device_id_type=MESH,
         )
 
     def collect(which):
-        all_rows(which).wait_recv()
+        all_lines(which).wait_recv()
         return gathered[which]
 
     one_row = lax.broadcasted_iota(jnp.int32, (1, height), 1)
@@ -532,7 +562,7 @@
         advection = u * xy[:points, lanes] + v * xy[points : 2 * points, lanes] + w * z[rows, :height]
         friction = xy[2 * points :, lanes] * weight_z + weight_xy * z[rows, height:]
         rates.append(mass * (forcing[part] - advection) - viscosity * friction)
-    pl.semaphore_wait(barrier, devices - 1)
+    pl.semaphore_wait(barrier, greetings)
     rates = start(0, rates)
 
     for load in loads[5:]:
@@ -555,6 +585,7 @@
     whole = start(1, [raw])
     spread(0, coarse_row(raw))
     residual = finish(1, whole)[0]
+    relay(0)
 
     local = start(2, [local_solve(residual)])
     coarse = coarse_solve(collect(0))
@@ -564,6 +595,7 @@
     spread(1, with_scalars(coarse_row(raw), residual, first, raw))
     first_gradient = stage(4, first_gradient, 1)
     image = finish(3, image)[0]
+    relay(1)
 
     local = start(4, [local_solve(image)])
     rows = collect(1)
@@ -575,6 +607,7 @@
     raw, second_gradient = operate(second)
     spread(2, with_scalars(jnp.zeros((1, height), F32), residual, second, raw))
     second_gradient = start(5, second_gradient)
+    relay(2)
     gradients = join(1, old_gradient, 1) + join(4, first_gradient, 1)
     gamma, delta = scalars(collect(2))
     ratio = gamma / gamma_first
@@ -592,7 +625,8 @@
         for copy in copies(which):
             copy.wait_send()
     for which in range(GATHERS):
-        all_rows(which).wait_send()
+        line_rows(which).wait_send()
+        all_lines(which).wait_send()
 
 
 def on_device(flow_state, building_height, pressure_old):
@@ -628,9 +662,12 @@
     scratch += [pltpu.VMEM((4, number, height), F32) for number in EXCHANGES]
     scratch += [
         pltpu.VMEM((GATHERS, 1, height), F32),
+        pltpu.VMEM((GATHERS, parts[1], height), F32),
         pltpu.VMEM((GATHERS, devices, height), F32),
         pltpu.SemaphoreType.DMA((len(EXCHANGES), 8)),
         pltpu.SemaphoreType.DMA((len(EXCHANGES), 8)),
+        pltpu.SemaphoreType.DMA((GATHERS,)),
+        pltpu.SemaphoreType.DMA((GATHERS,)),
         pltpu.SemaphoreType.DMA((GATHERS,)),
         pltpu.SemaphoreType.DMA((GATHERS,)),
     ]
@@ -638,8 +675,8 @@
     state, pressure = pl.pallas_call(
         functools.partial(kernel, parts),
         out_shape=(
-            jax.ShapeDtypeStruct((components * points, height), F32),
-            jax.ShapeDtypeStruct((points, height), F32),
+            pltpu.VMEM((components * points, height), F32),
+            pltpu.VMEM((points, height), F32),
         ),
         in_specs=[pl.BlockSpec(memory_space=pltpu.HBM)] * len(operands),
         out_specs=(whole, whole),

time: 40.1 us -> 40.1 us (level)
  local copies, waits for them, and re-layouts: 2.19 us -> 1.27 us
  Pallas kernels: 36.5 us -> 37.4 us
    unnamed x4 -> x2, local copies, waits for them, and re-layouts: 2.19 us -> 1.27 us
    pallas_call x1, Pallas kernels: 36.5 us -> 37.4 us  [on_device(): pl.pallas_call(functools.partial(kernel, parts), out_shape=(pltpu.VMEM((c...]
where the time goes in v4:
time: 40.1 us; the launch traced here: 39.9 us
  Pallas kernels  37.4 us (93%)
  between operations  1.28 us (3%)
  local copies, waits for them, and re-layouts  1.27 us (3%)
    pallas_call x1, Pallas kernels, on_device(): pl.pallas_call(functools.partial(kernel, parts), out_shape=(pltpu.VMEM((c...  37.4 us
    unnamed x2, local copies, waits for them, and re-layouts  1.27 us

profile of v4, /device:TPU:0, one launch (start us, length us, event | category | flops | bytes accessed | tf_op | source)
XLA Modules:
  0.0 39.9 jit_solution(3154302035405334049)
XLA Ops:
  1.3 37.4 %shard_map.122 = (f32[256,128]{1,0:T(8,128)S(1)}, f32[64,128]{1,0:T(8,128)S(1)}) custom-call(f32[256,128]{1,0:T(8,128)} %bitcast.6, bf16[192,320]{1,0:T(8,128)(2,1)} %constant.16.clone.refs_1_, bf16[640,384]{1,0:T(8,128)(2,1)} %constant.17.clone.refs_2_, f32[576,128]{1,0:T(8,128)} %constant.20.clone.refs_3_, s32[1,1]{1,0:T(1,128)S(6)} %copy.17.refs_4_, ...), custom_call_target="tpu_custom_call" | custom-call | tf_op jit(solution)/shard_map/pallas_call | solution.py:675
  38.6 0.7 %copy.15 = f32[4,8,8,128]{3,2,1,0:T(8,128)} copy(f32[4,8,8,128]{3,2,1,0:T(8,128)S(1)} %bitcast.4) | data formatting | bytes 262144
  39.3 0.6 %copy.16 = f32[8,8,128]{2,1,0:T(8,128)} copy(f32[8,8,128]{2,1,0:T(8,128)S(1)} %bitcast.5) | data formatting | bytes 65536

commit v5 on v3

--- a/solution.py
+++ b/solution.py
@@ -326,8 +326,8 @@
         return product(stacked, right_ref[:, first * height : last * height])
 
     lane = lax.broadcasted_iota(jnp.int32, (points, height), 1)
-    joins_up = (lax.rem(lane, N) == N - 1) & (lane < height - 1)
-    joins_down = (lax.rem(lane, N) == 0) & (lane > 0)
+    joins_up = ((lane & (N - 1)) == N - 1) & (lane < height - 1)
+    joins_down = ((lane & (N - 1)) == 0) & (lane > 0)
 
     def pair_z(values):
         up = pltpu.roll(values, height - 1, 1)
@@ -442,11 +442,14 @@
     spare = height // N + 1
 
     def operate(values):
-        xy = left_exact(values, DX, KXY + 1)
-        z = right_exact(values, ZD, ZK + 1)
-        image = xy[2 * points :] * weight_z + weight_xy * z[:, height:]
-        gradient = [mass * xy[:points], mass * xy[points : 2 * points], mass * z[:, :height]]
-        return image + helmholtz_shift * mass * values, gradient
+        image = left_exact(values, KXY, KXY + 1) * weight_z
+        image = image + weight_xy * right_exact(values, ZK, ZK + 1)
+        return image + helmholtz_shift * mass * values
+
+    def gradient(values):
+        xy = left_exact(values, DX, DY + 1)
+        z = right_exact(values, ZD, ZD + 1)
+        return [mass * xy[:points], mass * xy[points:], mass * z]
 
     def coarse_row(part):
         high, low, rest = split_thrice(part)
@@ -522,7 +525,7 @@
     u, v, w, theta = flow
     xy = left_exact(jnp.concatenate(flow, axis=1), DX, KXY + 1)
     z = right_exact(flow_ref[...], ZD, ZK + 1)
-    canopy = jnp.where(lane // N < roof_ref[...], 1.0, 0.0)
+    canopy = jnp.where(lane < N * roof_ref[...], 1.0, 0.0)
     drag = drag_strength * canopy * jnp.sqrt(u * u + v * v + w * w)
     forcing = [-drag * u, -drag * v, -drag * w + buoyancy * theta, heating * canopy]
     rates = []
@@ -538,8 +541,8 @@
     for load in loads[5:]:
         load.wait()
     old = old_ref[...]
-    old_image, old_gradient = operate(old)
-    old_gradient = stage(1, old_gradient, 1)
+    old_image = operate(old)
+    old_gradient = stage(1, gradient(old), 1)
     own = own_modes(0) if pieces == 1 else None
 
     rates = finish(0, rates)
@@ -559,10 +562,10 @@
     local = start(2, [local_solve(residual)])
     coarse = coarse_solve(collect(0))
     first = finish(2, local)[0] + coarse
-    raw, first_gradient = operate(first)
+    raw = operate(first)
     image = start(3, [raw])
     spread(1, with_scalars(coarse_row(raw), residual, first, raw))
-    first_gradient = stage(4, first_gradient, 1)
+    first_gradient = stage(4, gradient(first), 1)
     image = finish(3, image)[0]
 
     local = start(4, [local_solve(image)])
@@ -572,9 +575,9 @@
     alpha_first = gamma_first / delta_first
     residual = residual - alpha_first * image
     second = first - alpha_first * (finish(4, local)[0] + coarse)
-    raw, second_gradient = operate(second)
+    raw = operate(second)
     spread(2, with_scalars(jnp.zeros((1, height), F32), residual, second, raw))
-    second_gradient = start(5, second_gradient)
+    second_gradient = start(5, gradient(second))
     gradients = join(1, old_gradient, 1) + join(4, first_gradient, 1)
     gamma, delta = scalars(collect(2))
     ratio = gamma / gamma_first
@@ -638,8 +641,8 @@
     state, pressure = pl.pallas_call(
         functools.partial(kernel, parts),
         out_shape=(
-            jax.ShapeDtypeStruct((components * points, height), F32),
-            jax.ShapeDtypeStruct((points, height), F32),
+            pltpu.VMEM((components * points, height), F32),
+            pltpu.VMEM((points, height), F32),
         ),
         in_specs=[pl.BlockSpec(memory_space=pltpu.HBM)] * len(operands),
         out_specs=(whole, whole),

time: 40.1 us -> 38.6 us (0.963)
  local copies, waits for them, and re-layouts: 2.19 us -> 1.27 us
  Pallas kernels: 36.5 us -> 35.9 us
    unnamed x4 -> x2, local copies, waits for them, and re-layouts: 2.19 us -> 1.27 us
    pallas_call x1, Pallas kernels: 36.5 us -> 35.9 us  [on_device(): pl.pallas_call(functools.partial(kernel, parts), out_shape=(pltpu.VMEM((c...]
where the time goes in v5:
time: 38.6 us; the launch traced here: 38.4 us
  Pallas kernels  35.9 us (93%)
  between operations  1.28 us (3%)
  local copies, waits for them, and re-layouts  1.27 us (3%)
    pallas_call x1, Pallas kernels, on_device(): pl.pallas_call(functools.partial(kernel, parts), out_shape=(pltpu.VMEM((c...  35.9 us
    unnamed x2, local copies, waits for them, and re-layouts  1.27 us

profile of v5, /device:TPU:0, one launch (start us, length us, event | category | flops | bytes accessed | tf_op | source)
XLA Modules:
  0.0 38.4 jit_solution(4413914730344434068)
XLA Ops:
  1.3 35.9 %shard_map.122 = (f32[256,128]{1,0:T(8,128)S(1)}, f32[64,128]{1,0:T(8,128)S(1)}) custom-call(f32[256,128]{1,0:T(8,128)} %bitcast.6, bf16[192,320]{1,0:T(8,128)(2,1)} %constant.16.clone.refs_1_, bf16[640,384]{1,0:T(8,128)(2,1)} %constant.17.clone.refs_2_, f32[576,128]{1,0:T(8,128)} %constant.20.clone.refs_3_, s32[1,1]{1,0:T(1,128)S(6)} %copy.17.refs_4_, ...), custom_call_target="tpu_custom_call" | custom-call | tf_op jit(solution)/shard_map/pallas_call | solution.py:641
  37.1 0.7 %copy.15 = f32[4,8,8,128]{3,2,1,0:T(8,128)} copy(f32[4,8,8,128]{3,2,1,0:T(8,128)S(1)} %bitcast.4) | data formatting | bytes 262144
  37.8 0.6 %copy.16 = f32[8,8,128]{2,1,0:T(8,128)} copy(f32[8,8,128]{2,1,0:T(8,128)S(1)} %bitcast.5) | data formatting | bytes 65536

commit v6 on v5

--- a/solution.py
+++ b/solution.py
@@ -229,7 +229,7 @@
     return jnp.dot(first, second, preferred_element_type=F32)
 
 
-EXCHANGES = (4, 4, 1, 1, 4, 3)
+EXCHANGES = (4, 4, 1, 1, 1, 6)
 GATHERS = 3
 OPERANDS = 11
 
@@ -337,13 +337,13 @@
     def copies(which):
         field = fields[which]
         plan = []
-        x_faces = (field.at[:, points - N : points, :], field.at[:, 0:N, :])
-        for side, target in ((0, after_x), (1, before_x)):
-            plan.append((x_faces[side], x_in[which].at[side], (target, my_y)))
         for corner, target in enumerate(
             ((after_x, after_y), (after_x, before_y), (before_x, after_y), (before_x, before_y))
         ):
             plan.append((c_out[which].at[corner], c_in[which].at[corner], target))
+        x_faces = (field.at[:, points - N : points, :], field.at[:, 0:N, :])
+        for side, target in ((0, after_x), (1, before_x)):
+            plan.append((x_faces[side], x_in[which].at[side], (target, my_y)))
         for side, target in ((0, after_y), (1, before_y)):
             plan.append((y_out[which].at[side], y_in[which].at[side], (my_x, target)))
         return [
@@ -565,27 +565,30 @@
     raw = operate(first)
     image = start(3, [raw])
     spread(1, with_scalars(coarse_row(raw), residual, first, raw))
-    first_gradient = stage(4, gradient(first), 1)
     image = finish(3, image)[0]
 
     local = start(4, [local_solve(image)])
+    first_gradient = stage(5, gradient(first))
     rows = collect(1)
     coarse = coarse_solve(rows)
     gamma_first, delta_first = scalars(rows)
     alpha_first = gamma_first / delta_first
     residual = residual - alpha_first * image
     second = first - alpha_first * (finish(4, local)[0] + coarse)
-    raw = operate(second)
+    raw, second_gradient = operate(second), gradient(second)
     spread(2, with_scalars(jnp.zeros((1, height), F32), residual, second, raw))
-    second_gradient = start(5, gradient(second))
-    gradients = join(1, old_gradient, 1) + join(4, first_gradient, 1)
+    second_gradient = stage(5, second_gradient, 3)
+    for copy in copies(5):
+        copy.start()
+    gradients = join(1, old_gradient, 1)
     gamma, delta = scalars(collect(2))
     ratio = gamma / gamma_first
     alpha = gamma / (delta - ratio * gamma / alpha_first)
     weight_first = alpha_first + alpha * ratio
     pressure_ref[...] = old + weight_first * first + alpha * second
     state_ref[3 * points : 4 * points, :] = provisional[3]
-    second_gradient = finish(5, second_gradient)
+    gradients += finish(5, first_gradient)
+    second_gradient = join(5, second_gradient, 3)
     inverse = block(INVERSE)
     for part in range(3):
         total = gradients[part] + weight_first * gradients[3 + part] + alpha * second_gradient[part]

time: 38.6 us -> 37 us (0.959)
  Pallas kernels: 35.9 us -> 34.3 us
    pallas_call x1, Pallas kernels: 35.9 us -> 34.3 us  [on_device(): pl.pallas_call(functools.partial(kernel, parts), out_shape=(pltpu.VMEM((c...]
where the time goes in v6:
time: 37 us; the launch traced here: 36.8 us
  Pallas kernels  34.3 us (93%)
  between operations  1.28 us (3%)
  local copies, waits for them, and re-layouts  1.27 us (3%)
    pallas_call x1, Pallas kernels, on_device(): pl.pallas_call(functools.partial(kernel, parts), out_shape=(pltpu.VMEM((c...  34.3 us
    unnamed x2, local copies, waits for them, and re-layouts  1.27 us

profile of v6, /device:TPU:0, one launch (start us, length us, event | category | flops | bytes accessed | tf_op | source)
XLA Modules:
  0.0 36.8 jit_solution(5707382714489972563)
XLA Ops:
  1.3 34.3 %shard_map.122 = (f32[256,128]{1,0:T(8,128)S(1)}, f32[64,128]{1,0:T(8,128)S(1)}) custom-call(f32[256,128]{1,0:T(8,128)} %bitcast.6, bf16[192,320]{1,0:T(8,128)(2,1)} %constant.16.clone.refs_1_, bf16[640,384]{1,0:T(8,128)(2,1)} %constant.17.clone.refs_2_, f32[576,128]{1,0:T(8,128)} %constant.20.clone.refs_3_, s32[1,1]{1,0:T(1,128)S(6)} %copy.17.refs_4_, ...), custom_call_target="tpu_custom_call" | custom-call | tf_op jit(solution)/shard_map/pallas_call | solution.py:644
  35.6 0.7 %copy.15 = f32[4,8,8,128]{3,2,1,0:T(8,128)} copy(f32[4,8,8,128]{3,2,1,0:T(8,128)S(1)} %bitcast.4) | data formatting | bytes 262144
  36.2 0.6 %copy.16 = f32[8,8,128]{2,1,0:T(8,128)} copy(f32[8,8,128]{2,1,0:T(8,128)S(1)} %bitcast.5) | data formatting | bytes 65536
